TPU v7x, 128 devices: a whole 4x4x4 slice. The times are simulated.
128 devices in a mesh: ctx: 32 (over x, z, y_lo), head: 4 (over y_hi, core).
Axes of the slice: x: 4, y: 4 (y_hi: 2, y_lo: 2; y = y_hi * 2 + y_lo), z: 4, core: 2. Of those that a mesh axis runs over, the one named last changes fastest.
Arguments:
- query_rows: bfloat16 [8192, 4096], P(('ctx', 'head')), may hold values from -12 to 12
- key_rows: bfloat16 [8192, 512], P('ctx', 'head'), may hold values from -12 to 12
- value_rows: bfloat16 [8192, 512], P('ctx', 'head'), may hold values from -6 to 6
- attn_output: bfloat16 [8192, 4096], P(('ctx', 'head')), may hold values from -3 to 3
- out_grad: bfloat16 [8192, 4096], P(('ctx', 'head')), may hold values from -6 to 6
- segments: int32 [8192], replicated, may hold values from 0 to 1, never falling along the last dimension, each value on 1 to 6144 neighbouring positions
- parents: int32 [64], replicated, may hold values from -1 to 62, as said below
Outputs:
- query_grad: bfloat16 [8192, 4096], P(('ctx', 'head'))
- key_grad: bfloat16 [8192, 512], P('ctx', 'head')
- value_grad: bfloat16 [8192, 512], P('ctx', 'head')
Inputs may be any that keep to these rules, and one draw needn't show every extreme that they name: parents[0] is -1; each block b with 0 < b < 32 has parent b - 1; each later block's parent is b - 1 or a block of the first half at least b - 32; the last block's parent is the block before it.
All inputs are finite; a program needn't handle non-finite values.
Results may differ from a plain program's by a relative error of at most 0.005.
Values may be sent and summed in bfloat16 or wider, within the bound.
A program may use at most 64 MiB of HBM per device.

v0:
```python
import math

import jax
import jax.numpy as jnp
from jax import lax
from jax.sharding import PartitionSpec as P

D_HEAD = 128
Q_HEADS = 32
KV_HEADS = 4
BLOCK = 128


NEG = -1e30


def ancestors(parents):
    blocks_total = parents.shape[0]
    block_ids = jnp.arange(blocks_total, dtype=jnp.int32)
    reachable = (
        (block_ids[:, None] == block_ids[None, :]) | (parents[:, None] == block_ids[None, :])
    ).astype(jnp.int32)
    for squaring in range(max(1, (blocks_total - 1).bit_length())):
        reachable = (jnp.matmul(reachable, reachable) > 0).astype(jnp.int32)
    return reachable


def local(query_rows, key_rows, value_rows, attn_output, out_grad, segments, parents):
    ctx_size = lax.axis_size("ctx")
    head_count = lax.axis_size("head")
    kv_local = KV_HEADS // head_count
    group_size = Q_HEADS // KV_HEADS
    tok_dev = key_rows.shape[0]
    token_count = tok_dev * ctx_size
    score_scale = 1.0 / math.sqrt(D_HEAD)
    queries, grads_out, outputs = (
        lax.all_to_all(query_rows, "head", split_axis=1, concat_axis=0, tiled=True),
        lax.all_to_all(out_grad, "head", split_axis=1, concat_axis=0, tiled=True),
        lax.all_to_all(attn_output, "head", split_axis=1, concat_axis=0, tiled=True),
    )
    products = grads_out.astype(jnp.float32) * outputs.astype(jnp.float32)
    out_dot = jnp.sum(products.reshape(tok_dev, kv_local * group_size, D_HEAD), axis=-1)
    query_four = queries.reshape(tok_dev, kv_local, group_size, D_HEAD)
    grad_four = grads_out.reshape(tok_dev, kv_local, group_size, D_HEAD)
    out_dot = jnp.transpose(out_dot.reshape(tok_dev, kv_local, group_size), (1, 2, 0))
    ctx_index = lax.axis_index("ctx")
    query_start = ctx_index * tok_dev
    reachable = ancestors(parents)
    query_blocks = lax.dynamic_slice_in_dim(reachable, query_start // BLOCK, tok_dev // BLOCK, 0)
    query_blocks = jnp.repeat(query_blocks, BLOCK, axis=0)
    query_segments = lax.dynamic_slice_in_dim(segments, query_start, tok_dev, 0)
    query_positions = query_start + jnp.arange(tok_dev, dtype=jnp.int32)

    def allowed_for(key_start, width):
        block_cols = lax.dynamic_slice_in_dim(query_blocks, key_start // BLOCK, width // BLOCK, 1)
        block_cols = jnp.repeat(block_cols, BLOCK, axis=1)
        key_segments = lax.dynamic_slice_in_dim(segments, key_start, width, 0)
        key_positions = key_start + jnp.arange(width, dtype=jnp.int32)
        return (
            (block_cols > 0)
            & (query_segments[:, None] == key_segments[None, :])
            & (key_positions[None, :] <= query_positions[:, None])
        )

    def scores_for(key_block):
        return (
            jnp.einsum("qkgd,jkd->kgqj", query_four, key_block, preferred_element_type=jnp.float32)
            * score_scale
        )

    def stats_update(running, key_block, allowed):
        row_max = running[0]
        row_sum = running[1]
        masked = jnp.where(allowed, scores_for(key_block), NEG)
        new_max = jnp.maximum(row_max, jnp.max(masked, axis=-1))
        fresh = jnp.sum(jnp.where(allowed, jnp.exp(masked - new_max[..., None]), 0.0), axis=-1)
        return (new_max, row_sum * jnp.exp(row_max - new_max) + fresh)

    def grad_terms(key_block, value_block, allowed, log_total):
        masked = jnp.where(allowed, scores_for(key_block), NEG)
        weights = jnp.where(allowed, jnp.exp(masked - log_total[..., None]), 0.0)
        weights_half = weights.astype(jnp.bfloat16)
        weight_grad = jnp.einsum(
            "qkgd,jkd->kgqj", grad_four, value_block, preferred_element_type=jnp.float32
        )
        score_grad = (weights * (weight_grad - out_dot[..., None])).astype(jnp.bfloat16)
        query_term = jnp.einsum(
            "kgqj,jkd->qkgd", score_grad, key_block, preferred_element_type=jnp.float32
        )
        key_term = (
            jnp.einsum("kgqj,qkgd->jkd", score_grad, query_four, preferred_element_type=jnp.float32)
            * score_scale
        )
        value_term = jnp.einsum(
            "kgqj,qkgd->jkd", weights_half, grad_four, preferred_element_type=jnp.float32
        )
        return (query_term, key_term, value_term)

    start_max = jnp.full((kv_local, group_size, tok_dev), NEG, jnp.float32)
    start_sum = jnp.zeros((kv_local, group_size, tok_dev), jnp.float32)
    query_zero = jnp.zeros((tok_dev, kv_local, group_size, D_HEAD), jnp.float32)
    key_all, value_all = (
        lax.all_gather(key_rows, "ctx", axis=0, tiled=True),
        lax.all_gather(value_rows, "ctx", axis=0, tiled=True),
    )
    key_all = key_all.reshape(token_count, kv_local, D_HEAD)
    value_all = value_all.reshape(token_count, kv_local, D_HEAD)
    width = math.gcd(token_count, 512)
    block_total = token_count // width

    def stats_turn(block_index, running):
        key_start = block_index * width
        key_block = lax.dynamic_slice_in_dim(key_all, key_start, width, 0)
        return stats_update(running, key_block, allowed_for(key_start, width))

    row_max, row_sum = lax.fori_loop(0, block_total, stats_turn, (start_max, start_sum))
    log_total = row_max + jnp.log(row_sum)

    def grad_turn(query_acc, block_index):
        key_start = block_index * width
        key_block = lax.dynamic_slice_in_dim(key_all, key_start, width, 0)
        value_block = lax.dynamic_slice_in_dim(value_all, key_start, width, 0)
        query_term, key_term, value_term = grad_terms(
            key_block, value_block, allowed_for(key_start, width), log_total
        )
        return (query_acc + query_term, (key_term, value_term))

    query_acc, (key_terms, value_terms) = lax.scan(
        grad_turn, query_zero, jnp.arange(block_total, dtype=jnp.int32)
    )
    key_terms = key_terms.reshape(token_count, kv_local * D_HEAD)
    value_terms = value_terms.reshape(token_count, kv_local * D_HEAD)
    key_sum, value_sum = (
        lax.psum_scatter(key_terms, "ctx", scatter_dimension=0, tiled=True),
        lax.psum_scatter(value_terms, "ctx", scatter_dimension=0, tiled=True),
    )
    key_grad = key_sum.astype(jnp.bfloat16)
    value_grad = value_sum.astype(jnp.bfloat16)
    query_local = (
        (query_acc * score_scale)
        .astype(jnp.bfloat16)
        .reshape(tok_dev, kv_local * group_size * D_HEAD)
    )
    query_grad = lax.all_to_all(query_local, "head", split_axis=0, concat_axis=1, tiled=True)
    return (query_grad, key_grad, value_grad)


def solution(mesh):
    placed = (
        P(("ctx", "head"), None),
        P("ctx", "head"),
        P("ctx", "head"),
        P(("ctx", "head"), None),
        P(("ctx", "head"), None),
        P(),
        P(),
    )
    return jax.shard_map(
        local,
        mesh=mesh,
        in_specs=placed,
        out_specs=(P(("ctx", "head"), None), P("ctx", "head"), P("ctx", "head")),
        check_vma=False,
    )
```

profile of v0, /device:TPU:0, one launch (start us, length us, event | category | flops | bytes accessed | tf_op | source)
XLA Modules:
  0.0 862.1 jit_solution(7799265125038477698)
XLA Ops:
  9.8 4.5 all-to-all-start
  16.2 9.9 %all-to-all-done = bf16[64,4,1024]{2,0,1:T(8,128)(2,1)S(1)} async-done(((bf16[64,4,1024]{2,0,1:T(8,128)(2,1)}), bf16[64,4,1024]{2,0,1:T(8,128)(2,1)S(1)}, u32[]{:S(2)}, u32[]{:S(2)}) %all-to-all-start) | async-done | bytes 524320 | tf_op jit(solution)/shard_map/all_to_all | solution.py:37
  26.1 3.5 all-to-all-start.1
  31.4 11.7 %all-to-all-done.1 = bf16[64,4,1024]{2,0,1:T(8,128)(2,1)S(1)} async-done(((bf16[64,4,1024]{2,0,1:T(8,128)(2,1)}), bf16[64,4,1024]{2,0,1:T(8,128)(2,1)S(1)}, u32[]{:S(2)}, u32[]{:S(2)}) %all-to-all-start.1) | async-done | bytes 524320 | tf_op jit(solution)/shard_map/all_to_all | solution.py:38
  43.0 3.5 all-to-all-start.2
  48.5 11.5 %all-to-all-done.2 = bf16[64,4,1024]{2,0,1:T(8,128)(2,1)S(1)} async-done(((bf16[64,4,1024]{2,0,1:T(8,128)(2,1)}), bf16[64,4,1024]{2,0,1:T(8,128)(2,1)S(1)}, u32[]{:S(2)}, u32[]{:S(2)}) %all-to-all-start.2) | async-done | bytes 524320 | tf_op jit(solution)/shard_map/all_to_all | solution.py:39
  61.0 105.1 %all-gather.3.cloned.1.call-done = bf16[8192,128]{1,0:T(8,128)(2,1)} async-done(((bf16[256,128]{1,0:T(8,128)(2,1)}), bf16[8192,128]{1,0:T(8,128)(2,1)}) %all-gather.3.cloned.1.call-update) | async-done | bytes 2097168 | tf_op jit(solution)/shard_map/all_gather | solution.py:103
  166.0 127.0 %while.35 = (s32[]{:T(128)}, f32[1,8,256]{2,1,0:T(8,128)S(1)}, f32[1,8,256]{2,1,0:T(8,128)S(1)}, s32[256,64]{0,1:T(8,128)S(1)}, s32[256]{0:T(256)S(1)}, /*index=...) while((s32[]{:T(128)}, f32[1,8,256]{2,1,0:T(8,128)S(1)}, ...), condition=%wide.region_3.4_spmd.clone, body=%wide.region_0.3_spmd.clone.sunk | while | flops 277360416 | bytes 9563545 | solution.py:116
  167.0 3.7 fusion.100
  170.7 3.2 select_reduce_fusion.2
  175.0 3.7 fusion.100
  178.6 3.2 select_reduce_fusion.2
  182.9 3.6 fusion.100
  186.6 3.2 select_reduce_fusion.2
  190.8 3.7 fusion.100
  194.5 3.2 select_reduce_fusion.2
  198.8 3.7 fusion.100
  202.4 3.2 select_reduce_fusion.2
  206.7 3.7 fusion.100
  210.4 3.2 select_reduce_fusion.2
  214.7 3.7 fusion.100
  218.3 3.2 select_reduce_fusion.2
  222.6 3.7 fusion.100
  226.3 3.2 select_reduce_fusion.2
  230.6 3.7 fusion.100
  234.2 3.2 select_reduce_fusion.2
  238.5 3.7 fusion.100
  242.2 3.2 select_reduce_fusion.2
  246.5 3.6 fusion.100
  250.1 3.2 select_reduce_fusion.2
  254.4 3.7 fusion.100
  258.1 3.2 select_reduce_fusion.2
  262.3 3.7 fusion.100
  266.0 3.2 select_reduce_fusion.2
  270.3 3.6 fusion.100
  273.9 3.2 select_reduce_fusion.2
  278.2 3.7 fusion.100
  281.9 3.2 select_reduce_fusion.2
  286.2 3.7 fusion.100
  289.8 3.2 select_reduce_fusion.2
  293.1 27.4 %all-gather.5.cloned.1.call-done = bf16[8192,128]{1,0:T(8,128)(2,1)} async-done(((bf16[256,128]{1,0:T(8,128)(2,1)}), bf16[8192,128]{1,0:T(8,128)(2,1)}) %all-gather.5.cloned.1.call-update) | async-done | bytes 2097168 | tf_op jit(solution)/shard_map/all_gather | solution.py:104
  320.4 196.6 %while.36 = (s32[]{:T(128)}, f32[256,1,8,128]{0,3,2,1:T(8,128)}, f32[16,512,1,128]{3,1,2,0:T(8,128)}, f32[16,512,1,128]{3,1,2,0:T(8,128)}, s32[16]{0:T(128)S(1)}...) while((s32[]{:T(128)}, f32[256,1,8,128]{0,3,2,1:T(8,128)}, ...), condition=%wide.region_6.7_spmd.clone, body=%wide.region_5.6_spmd.clone.sunk | while | flops 1355876096 | bytes 24424924 | solution.py:128
  477.4 2.7 fusion.114
  489.7 2.7 fusion.114
  502.0 2.7 fusion.114
  519.0 20.3 %all_to_all.64 = bf16[4,64,1024]{2,1,0:T(8,128)(2,1)S(1)} all-to-all(bf16[4,64,1024]{2,1,0:T(8,128)(2,1)S(1)} %all_to_all.56), channel_id=1, replica_groups=mesh['ctx'=32,'head'=4] {'head'}, dimensions={0} | all-to-all | bytes 1048576 | tf_op jit(solution)/shard_map/all_to_all | solution.py:144
  540.1 146.2 %reduce-scatter.3.cloned.1.call-done = f32[256,128]{1,0:T(8,128)} async-done(((f32[8192,128]{1,0:T(8,128)}), f32[256,128]{1,0:T(8,128)}) %reduce-scatter.3.cloned.1.call-update) | async-done | bytes 131088 | tf_op jit(solution)/shard_map/reduce_scatter | solution.py:134
  687.8 166.2 %reduce-scatter.5.cloned.1.call-done = f32[256,128]{1,0:T(8,128)} async-done(((f32[8192,128]{1,0:T(8,128)}), f32[256,128]{1,0:T(8,128)}) %reduce-scatter.5.cloned.1.call-update) | async-done | bytes 131088 | tf_op jit(solution)/shard_map/reduce_scatter | solution.py:135
  (348 shorter events, 207.9 us)
Async XLA Ops:
  7.2 23.2 %copy-start.1 = (bf16[64,4096]{1,0:T(8,128)(2,1)S(1)}, bf16[64,4096]{1,0:T(8,128)(2,1)}, u32[]{:S(2)}) copy-start(bf16[64,4096]{1,0:T(8,128)(2,1)} %param.14) | copy-start | bytes 1572868
  7.2 24.0 %copy-start.2 = (s32[64]{0:T(128)S(1)}, s32[64]{0:T(128)}, u32[]{:S(2)}) copy-start(s32[64]{0:T(128)} %param.17) | copy-start | bytes 772
  7.2 158.9 %all-gather.3.cloned.1.call-start = ((), (), s32[]{:S(2)}) async-start(), calls=%async_computation.6 | async-start | bytes 2162688 | tf_op jit(solution)/shard_map/all_gather | solution.py:103
  9.8 16.3 %all-to-all-start = ((bf16[64,4,1024]{2,0,1:T(8,128)(2,1)}), bf16[64,4,1024]{2,0,1:T(8,128)(2,1)S(1)}, u32[]{:S(2)}, u32[]{:S(2)}) async-start(bf16[64,4,1024]{2,0,1:T(8,128)(2,1)} %bitcast.200), calls=%async_computation | async-start | bytes 1048576 | tf_op jit(solution)/shard_map/all_to_all | solution.py:37
  26.1 16.9 %all-to-all-start.1 = ((bf16[64,4,1024]{2,0,1:T(8,128)(2,1)}), bf16[64,4,1024]{2,0,1:T(8,128)(2,1)S(1)}, u32[]{:S(2)}, u32[]{:S(2)}) async-start(bf16[64,4,1024]{2,0,1:T(8,128)(2,1)} %bitcast.199), calls=%async_computation.1 | async-start | bytes 1048576 | tf_op jit(solution)/shard_map/all_to_all | solution.py:38
  29.6 290.9 %all-gather.5.cloned.1.call-start = ((), (), s32[]{:S(2)}) async-start(), calls=%async_computation.7 | async-start | bytes 2162688 | tf_op jit(solution)/shard_map/all_gather | solution.py:104
  43.0 17.0 %all-to-all-start.2 = ((bf16[64,4,1024]{2,0,1:T(8,128)(2,1)}), bf16[64,4,1024]{2,0,1:T(8,128)(2,1)S(1)}, u32[]{:S(2)}, u32[]{:S(2)}) async-start(bf16[64,4,1024]{2,0,1:T(8,128)(2,1)} %bitcast.198), calls=%async_computation.2 | async-start | bytes 1048576 | tf_op jit(solution)/shard_map/all_to_all | solution.py:39
  46.5 639.8 %reduce-scatter.3.cloned.1.call-start = ((), (), s32[]{:S(2)}) async-start(), calls=%async_computation.8 | async-start | bytes 4325376 | tf_op jit(solution)/shard_map/reduce_scatter | solution.py:134
  517.1 1.2 copy-start
  517.1 336.9 %reduce-scatter.5.cloned.1.call-start = ((), (), s32[]{:S(2)}) async-start(), calls=%async_computation.9 | async-start | bytes 4325376 | tf_op jit(solution)/shard_map/reduce_scatter | solution.py:135
Sparse Core Ops, SparseCore 0:
  9.7 156.3 all-gather.2
  167.7 152.7 all-gather.4
  517.2 169.0 reduce-scatter.2
  688.5 165.4 reduce-scatter.4
where the time goes:
time: 866 us; the launch traced here: 862 us
  waiting for transfers between devices  480 us (55%)
  matrix products  219 us (25%)
  other arithmetic  62.3 us (7%)
  local copies, waits for them, and re-layouts  42 us (5%)
  blocking collectives  20.3 us (2%)
  between operations  14 us (2%)
  loops' own time  12.8 us (1%)
  starting transfers between devices  11.7 us (1%)
    reduce_scatter x1, waiting for transfers between devices, local(): lax.psum_scatter(value_terms, 'ctx', scatter_dimension=0, tiled=True)  166 us
    reduce_scatter x1, waiting for transfers between devices, local(): lax.psum_scatter(key_terms, 'ctx', scatter_dimension=0, tiled=True)  146 us
    all_gather x1, waiting for transfers between devices, local(): lax.all_gather(key_rows, 'ctx', axis=0, tiled=True)  105 us
    dot_general x32, matrix products, scores_for(): jnp.einsum('qkgd,jkd->kgqj', query_four, key_block, preferred_element_typ...  84.3 us
    reduce_sum x16, other arithmetic, stats_update(): jnp.sum(jnp.where(allowed, jnp.exp(masked - new_max[..., None]), 0.0), ax...  51 us
    dot_general x16, matrix products, grad_terms(): jnp.einsum('kgqj,jkd->qkgd', score_grad, key_block, preferred_element_typ...  43.5 us
    dot_general x16, matrix products, grad_terms(): jnp.einsum('qkgd,jkd->kgqj', grad_four, value_block, preferred_element_ty...  38.5 us
    dot_general x16, matrix products, grad_terms(): jnp.einsum('kgqj,qkgd->jkd', weights_half, grad_four, preferred_element_t...  29.4 us
  transfers between devices with their start and end apart: 7, of which 7 were waited for; matrix products, arithmetic and copies ran while one was open for 16% of the time, Pallas kernels for 0%

commit v1 on v0

v1 whole, which is shorter than its diff:
```python
import functools
import math

import jax
import jax.numpy as jnp
from jax import lax
from jax.experimental import pallas as pl
from jax.experimental.pallas import tpu as pltpu
from jax.sharding import PartitionSpec as P

D = 128
BLOCK = 128
TOKENS = 8192
COLUMN = 512
SECTION = 2048
NEAR = 3
GROUP = 4
ROWS = 512
SCALE = 1.0 / math.sqrt(D)
LOG2E = math.log2(math.e)
NEG = -1e30
F32 = jnp.float32
BF16 = jnp.bfloat16
MESH = pl.DeviceIdType.MESH
NT = (((1,), (1,)), ((), ()))
TN = (((0,), (0,)), ((), ()))


class Place:
    def __init__(self):
        ctx = lax.axis_index("ctx")
        head = lax.axis_index("head")
        self.x = ctx // 8
        self.z = (ctx // 2) % 4
        self.ylo = ctx % 2
        self.yhi = head // 2
        self.core = head % 2
        self.y = self.yhi * 2 + self.ylo

    def at(self, x=None, z=None, ylo=None, yhi=None, core=None):
        x = self.x if x is None else x
        z = self.z if z is None else z
        ylo = self.ylo if ylo is None else ylo
        yhi = self.yhi if yhi is None else yhi
        core = self.core if core is None else core
        return ((x * 4 + z) * 2 + ylo, yhi * 2 + core)

    def in_column(self, t):
        return self.at(ylo=(t // 2) % 2, yhi=t // 4, core=t % 2)

    @property
    def own(self):
        return self.y * 2 + self.core

    def home_row(self, t=None):
        if t is None:
            return (self.ylo * 2 + self.yhi) * 128 + self.core * 64
        return (((t // 2) % 2) * 2 + t // 4) * 128 + (t % 2) * 64


def greet(place):
    barrier = pltpu.get_barrier_semaphore()
    for t in range(8):
        @pl.when(place.own != t)
        def _():
            pl.semaphore_signal(barrier, inc=1, device_id=place.in_column(t), device_id_type=MESH)
    for step in range(1, 4):
        pl.semaphore_signal(
            barrier, inc=1, device_id=place.at(x=(place.x + step) % 4), device_id_type=MESH)
        pl.semaphore_signal(
            barrier, inc=1, device_id=place.at(z=(place.z + step) % 4), device_id_type=MESH)
    pl.semaphore_wait(barrier, 13)


def rcopy(src, dst, send, recv, device):
    return pltpu.make_async_remote_copy(
        src_ref=src, dst_ref=dst, send_sem=send, recv_sem=recv,
        device_id=device, device_id_type=MESH)


class Sends:
    def __init__(self, sems):
        self.sems = sems
        self.items = []

    def start(self, cond, src, dst, recv, device):
        copy = rcopy(src, dst, self.sems.at[len(self.items)], recv, device)
        self.items.append((cond, copy))
        if cond is None:
            copy.start()
        else:
            pl.when(cond)(copy.start)

    def finish(self):
        for cond, copy in self.items:
            if cond is None:
                copy.wait_send()
            else:
                pl.when(cond)(copy.wait_send)


def spread_kernel(q_ref, do_ref, o_ref, k_ref, v_ref,
                  qg_ref, dog_ref, dg_ref, kv_ref,
                  dsrc, col_send, q_recv, do_recv, d_recv, local_sem,
                  first_send, first_recv, piece_send, prim_recv, sib_recv):
    place = Place()
    x, z, core = place.x, place.z, place.core
    greet(place)

    first_row = pl.multiple_of((x * 4 + z) * COLUMN + place.ylo * 256, 256)
    firsts = []
    for p, src in ((0, k_ref), (1, v_ref)):
        dst = kv_ref.at[p, pl.ds(first_row, 256), :]
        here = (place.ylo == core) & (core == p)
        away = jnp.logical_not(here)
        copy = rcopy(src, dst, first_send.at[p], first_recv.at[place.ylo],
                     place.at(ylo=core, core=p))
        local = pltpu.make_async_copy(src, dst, local_sem.at[3])
        pl.when(away)(copy.start)
        pl.when(here)(local.start)
        firsts.append((here, away, copy, local))

    my_row = pl.multiple_of(place.home_row(), 64)
    columns = Sends(col_send)
    locals_ = []
    for t in range(8):
        cols = pl.ds(t * ROWS, ROWS)
        for n, (src, dst, recv) in enumerate(
                ((q_ref, qg_ref, q_recv), (do_ref, dog_ref, do_recv))):
            target = dst.at[pl.ds(my_row, 64), :]
            columns.start(place.own != t, src.at[:, cols], target, recv.at[place.own],
                          place.in_column(t))
            local = pltpu.make_async_copy(src.at[:, cols], target, local_sem.at[n])
            pl.when(place.own == t)(local.start)
            locals_.append((place.own == t, local))

    lane = lax.broadcasted_iota(jnp.int32, (8, 128), 1)
    line = lax.broadcasted_iota(jnp.int32, (8, 128), 0)
    mine = (lane // 64) == core
    ones = jnp.ones((8, D), BF16)
    for t in range(8):
        tile = jnp.zeros((8, 128), F32)
        for r in range(4):
            cols = slice((t * 4 + r) * D, (t * 4 + r + 1) * D)
            prod = do_ref[:, cols].astype(F32) * o_ref[:, cols].astype(F32)
            high = prod.astype(BF16)
            low = (prod - high.astype(F32)).astype(BF16)
            row = (lax.dot_general(ones, high, NT, preferred_element_type=F32)
                   + lax.dot_general(ones, low, NT, preferred_element_type=F32))
            row = jnp.concatenate([row, row], axis=1)
            tile = jnp.where(mine & (line == r), row, tile)
        dsrc[t] = tile
    for t in range(8):
        target = dg_ref.at[place.own]
        columns.start(place.own != t, dsrc.at[t], target, d_recv.at[place.own],
                      place.in_column(t))
        local = pltpu.make_async_copy(dsrc.at[t], target, local_sem.at[2])
        pl.when(place.own == t)(local.start)
        locals_.append((place.own == t, local))

    for half in range(2):
        here = (place.ylo == core) & (place.ylo == half)
        wait = rcopy(k_ref, kv_ref.at[core, pl.ds(0, 256), :], first_send.at[0],
                     first_recv.at[half], place.at(core=1 - core))
        pl.when(jnp.logical_not(here))(wait.wait_recv)
    for here, away, copy, local in firsts:
        pl.when(here)(local.wait)

    def piece(p, xx, zz):
        return kv_ref.at[p, pl.ds(pl.multiple_of((xx * 4 + zz) * COLUMN, COLUMN), COLUMN), :]

    sibling = place.at(core=1 - core)

    def run(c):
        sends = Sends(piece_send)

        def share(cond, xx, zz):
            part = piece(c, xx, zz)
            sends.start(cond, part, part, sib_recv.at[xx * 4 + zz], sibling)

        def along_x(cond, xx, zz):
            part = piece(c, xx, zz)
            for d in (1, 2):
                ok = x + d <= 3
                ok = ok if cond is None else ok & cond
                sends.start(ok, part, part, prim_recv.at[xx * 4 + zz],
                            place.at(x=(x + d) % 4))

        def along_z(cond, xx, zz):
            part = piece(c, xx, zz)
            for d in (1, 3, 2):
                sends.start(cond, part, part, prim_recv.at[xx * 4 + zz],
                            place.at(z=(z + d) % 4))

        def arrive(cond, xx, zz):
            part = piece(c, xx, zz)
            wait = rcopy(part, part, piece_send.at[0], prim_recv.at[xx * 4 + zz], sibling)
            if cond is None:
                wait.wait_recv()
            else:
                pl.when(cond)(wait.wait_recv)

        if c == 0:
            along_z(None, x, z)
            along_x(None, x, z)
            share(None, x, z)
            for dz in (1, 3, 2):
                zz = (z + dz) % 4
                arrive(None, x, zz)
                along_x(None, x, zz)
                share(None, x, zz)
            for dz in (0, 1, 3, 2):
                zz = (z + dz) % 4
                for d in (1, 2):
                    xx = (x + 4 - d) % 4
                    arrive(x >= d, xx, zz)
                    share(x >= d, xx, zz)
        else:
            along_x(None, x, z)
            along_z(None, x, z)
            share(None, x, z)
            for d in (1, 2):
                xx = (x + 4 - d) % 4
                arrive(x >= d, xx, z)
                along_z(x >= d, xx, z)
                share(x >= d, xx, z)
            for d in range(NEAR):
                xx = (x + 4 - d) % 4
                for dz in (1, 3, 2):
                    zz = (z + dz) % 4
                    arrive(None if d == 0 else x >= d, xx, zz)
                    share(None if d == 0 else x >= d, xx, zz)
        for d in range(NEAR):
            xx = (x + 4 - d) % 4
            for zz in range(4):
                part = piece(1 - c, xx, zz)
                wait = rcopy(part, part, piece_send.at[0], sib_recv.at[xx * 4 + zz], sibling)
                pl.when(x >= d)(wait.wait_recv)
        sends.finish()

    pl.when(core == 0)(lambda: run(0))
    pl.when(core == 1)(lambda: run(1))

    for t in range(8):
        @pl.when(place.own != t)
        def _():
            row = place.home_row(t)
            for src, dst, recv in ((q_ref, qg_ref, q_recv), (do_ref, dog_ref, do_recv)):
                rcopy(src.at[:, pl.ds(0, ROWS)], dst.at[pl.ds(row, 64), :], col_send.at[0],
                      recv.at[t], place.in_column(t)).wait_recv()
            rcopy(dsrc.at[t], dg_ref.at[t], col_send.at[0], d_recv.at[t],
                  place.in_column(t)).wait_recv()
    for cond, local in locals_:
        pl.when(cond)(local.wait)
    columns.finish()
    for here, away, copy, local in firsts:
        pl.when(away)(copy.wait_send)


def grad_kernel(parents_ref, seg_ref, q_ref, do_ref, dg_ref, kv_ref,
                dkv_ref, dq_ref,
                acc, expd, keys, values, qr, dor, tops, listed):
    place = Place()
    column = place.x * 4 + place.z
    n0 = jnp.sum((seg_ref[...] == 0).astype(jnp.int32))
    factor = SCALE * LOG2E

    acc[...] = jnp.zeros_like(acc)

    def one_block(qb, carry):
        gb = column * 4 + qb
        q_start = gb * BLOCK
        lowest = jnp.where(q_start >= n0, n0, 0)

        def more(state):
            b, n = state
            return (b >= 0) & (b * BLOCK + (BLOCK - 1) >= lowest)

        def note(state):
            b, n = state
            listed[n] = b
            return (parents_ref[b], n + 1)

        _, count = lax.while_loop(more, note, (gb, jnp.int32(0)))
        for i in range(GROUP - 1):
            listed[count + i] = gb
        groups = (count + GROUP - 1) // GROUP

        row = pl.multiple_of(qb * BLOCK, BLOCK)
        q_rows = q_ref[pl.ds(row, BLOCK), :]
        do_rows = do_ref[pl.ds(row, BLOCK), :]
        for h in range(4):
            qr[h * D:(h + 1) * D, :] = q_rows[:, h * D:(h + 1) * D]
            dor[h * D:(h + 1) * D, :] = do_rows[:, h * D:(h + 1) * D]
        source = ((qb % 2) * 2 + qb // 2) * 2
        pair = dg_ref[source] + dg_ref[source + 1]
        out_dot = jnp.concatenate([pair[h:h + 1, :] for h in range(4)], axis=1)

        query_at = q_start + lax.broadcasted_iota(jnp.int32, (1, ROWS), 1) % BLOCK
        least = jnp.where(query_at >= n0, n0, 0)
        edge = jnp.where(q_start + BLOCK - 1 >= n0, n0, 0)

        def scores_turn(g, state):
            top, total = state
            base = pl.multiple_of(g * GROUP * BLOCK, GROUP * BLOCK)
            at = pl.ds(base, GROUP * BLOCK)
            masked = (g == 0) | (g * GROUP + GROUP > count)
            for i in range(GROUP):
                b = listed[g * GROUP + i]
                masked = masked | (b * BLOCK < edge)
                rows = pl.ds(pl.multiple_of(b * BLOCK, BLOCK), BLOCK)
                dest = pl.ds(pl.multiple_of(base + i * BLOCK, BLOCK), BLOCK)
                keys[dest, :] = kv_ref[0, rows, :]
                values[dest, :] = kv_ref[1, rows, :]
            expd[at, :] = lax.dot_general(keys[at, :], qr[...], NT, preferred_element_type=F32)

            @pl.when(masked)
            def _():
                for i in range(GROUP):
                    b = listed[g * GROUP + i]
                    start = jnp.where(g * GROUP + i < count, b * BLOCK, 2 * TOKENS)
                    dest = pl.ds(pl.multiple_of(base + i * BLOCK, BLOCK), BLOCK)
                    key_at = start + lax.broadcasted_iota(jnp.int32, (BLOCK, ROWS), 0)
                    ok = (key_at <= query_at) & (key_at >= least)
                    expd[dest, :] = jnp.where(ok, expd[dest, :], NEG)

            scores = expd[at, :]
            new_top = jnp.maximum(top, jnp.max(scores, axis=0, keepdims=True))
            e = jnp.exp2((scores - new_top) * factor)
            expd[at, :] = e
            tops[g] = jnp.broadcast_to(new_top, (8, ROWS))
            total = total * jnp.exp2((top - new_top) * factor) + jnp.sum(e, axis=0, keepdims=True)
            return (new_top, total)

        top, total = lax.fori_loop(
            0, groups, scores_turn,
            (jnp.full((1, ROWS), NEG, F32), jnp.zeros((1, ROWS), F32)))
        inverse = 1.0 / total

        def grad_turn(g, dqt):
            base = pl.multiple_of(g * GROUP * BLOCK, GROUP * BLOCK)
            at = pl.ds(base, GROUP * BLOCK)
            share = jnp.exp2((tops[g][0:1, :] - top) * factor) * inverse
            weights = expd[at, :] * share
            half = weights.astype(BF16)
            weight_grad = lax.dot_general(values[at, :], dor[...], NT, preferred_element_type=F32)
            score_grad = (weights * (weight_grad - out_dot)).astype(BF16)
            dv = jnp.dot(half, dor[...], preferred_element_type=F32)
            dk = jnp.dot(score_grad, qr[...], preferred_element_type=F32)
            for i in range(GROUP):
                b = listed[g * GROUP + i]
                rows = pl.ds(pl.multiple_of(b * BLOCK, BLOCK), BLOCK)
                acc[0, rows, :] += dk[i * BLOCK:(i + 1) * BLOCK, :]
                acc[1, rows, :] += dv[i * BLOCK:(i + 1) * BLOCK, :]
            return dqt + lax.dot_general(keys[at, :], score_grad, TN, preferred_element_type=F32)

        dqt = lax.fori_loop(0, groups, grad_turn, jnp.zeros((D, ROWS), F32))
        for h in range(4):
            part = dqt[:, h * D:(h + 1) * D].T * SCALE
            dq_ref[pl.ds(row, BLOCK), h * D:(h + 1) * D] = part.astype(BF16)
        return carry

    lax.fori_loop(0, 4, one_block, 0)
    dkv_ref[0] = (acc[0] * SCALE).astype(BF16)
    dkv_ref[1] = acc[1].astype(BF16)


def home_kernel(dkv_ref, dq_ref,
                qg_ref, kg_ref, vg_ref,
                own, sib, acc, snd, hop, rx, rz, rzz, rx2, done,
                col_send, q_recv, local_sem, own_sem, sib_send, sib_recv,
                send_sems, rx_recv, rz_recv, rzz_recv, rx2_recv, end_send, end_recv):
    place = Place()
    x, z, core = place.x, place.z, place.core
    greet(place)
    sibling = place.at(core=1 - core)

    def section(p, d):
        start = pl.multiple_of(((x + 4 - d) % 4) * SECTION, SECTION)
        return dkv_ref.at[p, pl.ds(start, SECTION), :]

    sib_copies = []
    own_copies = []
    for d in (2, 1, 0):
        copy = rcopy(section(1 - core, d), sib.at[d], sib_send.at[d], sib_recv.at[d], sibling)
        mine = pltpu.make_async_copy(section(core, d), own.at[d], own_sem.at[d])
        pl.when(x >= d)(copy.start)
        pl.when(x >= d)(mine.start)
        sib_copies.append((d, copy))
        own_copies.append((d, mine))

    columns = Sends(col_send)
    col = pl.multiple_of(place.own * ROWS, ROWS)
    target = qg_ref.at[:, pl.ds(col, ROWS)]
    for t in range(8):
        src = dq_ref.at[pl.ds(place.home_row(t), 64), :]
        columns.start(place.own != t, src, target, q_recv.at[place.own], place.in_column(t))
        pl.when(place.own == t)(pltpu.make_async_copy(src, target, local_sem.at[0]).start)

    for (d, copy), (_, mine) in zip(sib_copies, own_copies):
        @pl.when(x >= d)
        def _():
            mine.wait()
            copy.wait_recv()
            both = own[d].astype(F32) + sib[d].astype(F32)
            acc[d] = both
            snd[d] = both.astype(BF16)

    my_rows = pl.ds(pl.multiple_of(z * COLUMN, COLUMN), COLUMN)

    def finish(p, out_ref, total):
        done[...] = total.astype(BF16)
        for half in range(2):
            src = done.at[pl.ds(half * 256, 256), :]
            here = (place.ylo == half) & (core == place.ylo)
            copy = rcopy(src, out_ref, end_send.at[half], end_recv.at[p],
                         place.at(ylo=half, core=place.ylo))
            local = pltpu.make_async_copy(src, out_ref, local_sem.at[1])
            pl.when(here)(local.start)
            pl.when(jnp.logical_not(here))(copy.start)
            pl.when(here)(local.wait)
            pl.when(jnp.logical_not(here))(copy.wait_send)

    @pl.when(core == 0)
    def _():
        sends = Sends(send_sems)
        for d in (2, 1):
            sends.start(x >= d, snd.at[d], rx.at[d - 1], rx_recv.at[d - 1],
                        place.at(x=(x + 4 - d) % 4))
        for d in (1, 2):
            @pl.when(x + d <= 3)
            def _():
                rcopy(snd.at[d], rx.at[d - 1], send_sems.at[0], rx_recv.at[d - 1],
                      sibling).wait_recv()
                acc[0] += rx[d - 1].astype(F32)
        hop[...] = acc[0].astype(BF16)
        for d in (1, 3, 2):
            zz = (z + d) % 4
            src = hop.at[pl.ds(pl.multiple_of(zz * COLUMN, COLUMN), COLUMN), :]
            sends.start(None, src, rz.at[d - 1], rz_recv.at[d - 1], place.at(z=zz))
        total = acc[0, my_rows, :]
        for d in (1, 3, 2):
            rcopy(rz.at[d - 1], rz.at[d - 1], send_sems.at[0], rz_recv.at[d - 1],
                  sibling).wait_recv()
            total = total + rz[d - 1].astype(F32)
        finish(0, kg_ref, total)
        sends.finish()

    @pl.when(core == 1)
    def _():
        sends = Sends(send_sems)
        for e in (2, 1, 0):
            for d in (1, 3, 2):
                zz = (z + d) % 4
                src = snd.at[e, pl.ds(pl.multiple_of(zz * COLUMN, COLUMN), COLUMN), :]
                sends.start(x >= e, src, rzz.at[d - 1, e], rzz_recv.at[d - 1, e], place.at(z=zz))
        total = None
        for e in (2, 1, 0):
            @pl.when(x >= e)
            def _():
                part = acc[e, my_rows, :]
                for d in (1, 3, 2):
                    rcopy(rzz.at[d - 1, e], rzz.at[d - 1, e], send_sems.at[0],
                          rzz_recv.at[d - 1, e], sibling).wait_recv()
                    part = part + rzz[d - 1, e].astype(F32)
                if e == 0:
                    acc[0, my_rows, :] = part
                else:
                    hop[e * COLUMN:(e + 1) * COLUMN, :] = part.astype(BF16)
            if e > 0:
                sends.start(x >= e, hop.at[pl.ds(e * COLUMN, COLUMN), :], rx2.at[e - 1],
                            rx2_recv.at[e - 1], place.at(x=(x + 4 - e) % 4))
        for d in (1, 2):
            @pl.when(x + d <= 3)
            def _():
                rcopy(rx2.at[d - 1], rx2.at[d - 1], send_sems.at[0], rx2_recv.at[d - 1],
                      sibling).wait_recv()
                acc[0, my_rows, :] += rx2[d - 1].astype(F32)
        finish(1, vg_ref, acc[0, my_rows, :])
        sends.finish()

    for p, out_ref in ((0, kg_ref), (1, vg_ref)):
        here = (place.ylo == core) & (core == p)
        wait = rcopy(done.at[pl.ds(0, 256), :], out_ref, end_send.at[0], end_recv.at[p], sibling)
        pl.when(jnp.logical_not(here))(wait.wait_recv)
    for t in range(8):
        @pl.when(place.own != t)
        def _():
            src = dq_ref.at[pl.ds(0, 64), :]
            rcopy(src, qg_ref.at[:, pl.ds(t * ROWS, ROWS)], col_send.at[0], q_recv.at[t],
                  sibling).wait_recv()
    pltpu.make_async_copy(dq_ref.at[pl.ds(0, 64), :], target, local_sem.at[0]).wait()
    columns.finish()
    for d, copy in sib_copies:
        pl.when(x >= d)(copy.wait_send)


ANY = pl.BlockSpec(memory_space=pl.ANY)
VMEM = pl.BlockSpec(memory_space=pltpu.VMEM)
SMEM = pl.BlockSpec(memory_space=pltpu.SMEM)
DMA = pltpu.SemaphoreType.DMA
MIB = 1 << 20


def struct(shape, dtype):
    return jax.ShapeDtypeStruct(shape, dtype)


def spread(q, do, o, k, v):
    return pl.pallas_call(
        spread_kernel,
        out_shape=(struct((COLUMN, ROWS), BF16), struct((COLUMN, ROWS), BF16),
                   struct((8, 8, 128), F32), struct((2, TOKENS, D), BF16)),
        in_specs=[ANY, VMEM, VMEM, ANY, ANY],
        out_specs=(ANY, ANY, ANY, ANY),
        scratch_shapes=[
            pltpu.VMEM((8, 8, 128), F32),
            DMA((24,)), DMA((8,)), DMA((8,)), DMA((8,)), DMA((4,)),
            DMA((2,)), DMA((2,)), DMA((32,)), DMA((16,)), DMA((16,)),
        ],
        compiler_params=pltpu.CompilerParams(
            collective_id=0, has_side_effects=True, vmem_limit_bytes=16 * MIB),
        name="spread",
    )(q, do, o, k, v)


def grads(parents, seg, q, do, dg, kv):
    return pl.pallas_call(
        grad_kernel,
        out_shape=(struct((2, TOKENS, D), BF16), struct((COLUMN, ROWS), BF16)),
        in_specs=[SMEM, VMEM, VMEM, VMEM, VMEM, VMEM],
        out_specs=(VMEM, VMEM),
        scratch_shapes=[
            pltpu.VMEM((2, TOKENS, D), F32),
            pltpu.VMEM((48 * BLOCK, ROWS), F32),
            pltpu.VMEM((48 * BLOCK, D), BF16),
            pltpu.VMEM((48 * BLOCK, D), BF16),
            pltpu.VMEM((ROWS, D), BF16),
            pltpu.VMEM((ROWS, D), BF16),
            pltpu.VMEM((12, 8, ROWS), F32),
            pltpu.SMEM((64,), jnp.int32),
        ],
        compiler_params=pltpu.CompilerParams(vmem_limit_bytes=56 * MIB),
        name="grads",
    )(parents, seg, q, do, dg, kv)


def home(dkv, dq):
    return pl.pallas_call(
        home_kernel,
        out_shape=(struct((64, 4096), BF16), struct((256, D), BF16), struct((256, D), BF16)),
        in_specs=[ANY, ANY],
        out_specs=(ANY, ANY, ANY),
        scratch_shapes=[
            pltpu.VMEM((NEAR, SECTION, D), BF16),
            pltpu.VMEM((NEAR, SECTION, D), BF16),
            pltpu.VMEM((NEAR, SECTION, D), F32),
            pltpu.VMEM((NEAR, SECTION, D), BF16),
            pltpu.VMEM((SECTION, D), BF16),
            pltpu.VMEM((2, SECTION, D), BF16),
            pltpu.VMEM((3, COLUMN, D), BF16),
            pltpu.VMEM((3, NEAR, COLUMN, D), BF16),
            pltpu.VMEM((2, COLUMN, D), BF16),
            pltpu.VMEM((COLUMN, D), BF16),
            DMA((8,)), DMA((8,)), DMA((2,)), DMA((3,)), DMA((3,)), DMA((3,)),
            DMA((12,)), DMA((2,)), DMA((3,)), DMA((3, 3)), DMA((2,)), DMA((2,)), DMA((2,)),
        ],
        compiler_params=pltpu.CompilerParams(
            collective_id=1, has_side_effects=True, vmem_limit_bytes=32 * MIB),
        name="home",
    )(dkv, dq)


def local(query_rows, key_rows, value_rows, attn_output, out_grad, segments, parents):
    q, do, dg, kv = spread(query_rows, out_grad, attn_output, key_rows, value_rows)
    dkv, dq = grads(parents, segments.reshape(64, 128), q, do, dg, kv)
    return home(dkv, dq)


def solution(mesh):
    placed = (
        P(("ctx", "head"), None),
        P("ctx", "head"),
        P("ctx", "head"),
        P(("ctx", "head"), None),
        P(("ctx", "head"), None),
        P(),
        P(),
    )
    return jax.shard_map(
        local,
        mesh=mesh,
        in_specs=placed,
        out_specs=(P(("ctx", "head"), None), P("ctx", "head"), P("ctx", "head")),
        check_vma=False,
    )
```

time: 866 us -> 129 us (0.15)
  the two profiles are of different devices: /device:TPU:0 before, /device:TPU:10 now
where the time goes in v1:
time: 129 us
  Pallas kernels  114 us (88%)
  local copies, waits for them, and re-layouts  14.3 us (11%)
    pallas_call x1, Pallas kernels, home(): pl.pallas_call(home_kernel, out_shape=(struct((64, 4096), BF16), struct((...  58.9 us
    pallas_call x1, Pallas kernels, grads(): pl.pallas_call(grad_kernel, out_shape=(struct((2, TOKENS, D), BF16), stru...  32.7 us
    pallas_call x1, Pallas kernels, spread(): pl.pallas_call(spread_kernel, out_shape=(struct((COLUMN, ROWS), BF16), st...  22.5 us
    unnamed x25, local copies, waits for them, and re-layouts  14.3 us

profile of v1, /device:TPU:10, one launch (start us, length us, event | category | flops | bytes accessed | tf_op | source)
XLA Modules:
  0.0 128.9 jit_solution(5334017694959248114)
XLA Ops:
  0.6 0.0 copy-start.3
  0.6 1.0 copy-done.3
  1.7 0.0 copy-start.4
  1.7 1.0 copy-done.4
  2.7 0.0 copy-start.5
  2.7 1.0 copy-done.5
  3.8 0.0 copy-start.8
  3.8 0.8 copy-done.8
  4.6 0.0 copy-start.9
  4.6 0.8 copy-done.9
  5.4 22.5 %spread.1 = (bf16[512,512]{1,0:T(8,128)(2,1)S(1)}, bf16[512,512]{1,0:T(8,128)(2,1)S(1)}, f32[8,8,128]{2,1,0:T(8,128)S(1)}, bf16[2,8192,128]{2,1,0:T(8,128)(2,1)S(1)}) custom-call(bf16[64,4096]{1,0:T(8,128)(2,1)S(1)} %copy-done.3, bf16[64,4096]{1,0:T(8,128)(2,1)S(1)} %copy-done.4, bf16[64,4096]{1,0:T(8,128)(2,1)S(1)} %copy-done.5, ...), custom_call_target="tpu_custom_call" | custom-call | tf_op jit(solution)/shard_map/spread/pallas_call | solution.py:510
  27.9 0.0 copy-start.1
  27.9 1.9 %copy-done.1 = bf16[2,8192,128]{2,1,0:T(8,128)(2,1)} copy-done((bf16[2,8192,128]{2,1,0:T(8,128)(2,1)}, bf16[2,8192,128]{2,1,0:T(8,128)(2,1)S(1)}, u32[]{:S(2)}) %copy-start.1) | copy-done | bytes 4194328
  29.9 0.0 copy-start.6
  29.9 0.8 copy-done.6
  30.7 0.0 copy-start.7
  30.7 0.8 copy-done.7
  31.5 0.0 copy-start.10
  31.5 0.6 copy-done.10
  32.1 32.7 %grads.1 = (bf16[2,8192,128]{2,1,0:T(8,128)(2,1)}, bf16[512,512]{1,0:T(8,128)(2,1)}) custom-call(s32[64]{0:T(128)} %parents_ref.1, s32[64,128]{1,0:T(8,128)} %bitcast.1, bf16[512,512]{1,0:T(8,128)(2,1)} %copy-done.6, bf16[512,512]{1,0:T(8,128)(2,1)} %copy-done.7, f32[8,8,128]{2,1,0:T(8,128)} %copy-done.10, bf16[2,8192,128]{2,1,0:T(8,128)(2,1)} %copy-done.1), custom_call_target="tpu_custom_call" | custom-call | tf_op jit(solution)/shard_map/grads/pallas_call | solution.py:528
  64.8 0.0 copy-start
  64.8 2.2 %copy-done = bf16[2,8192,128]{2,1,0:T(8,128)(2,1)S(1)} copy-done((bf16[2,8192,128]{2,1,0:T(8,128)(2,1)S(1)}, bf16[2,8192,128]{2,1,0:T(8,128)(2,1)}, u32[]{:S(2)}) %copy-start) | copy-done | bytes 4194328
  67.0 0.0 copy-start.2
  67.0 1.0 copy-done.2
  68.0 58.9 %home.1 = (bf16[64,4096]{1,0:T(8,128)(2,1)S(1)}, bf16[256,128]{1,0:T(8,128)(2,1)S(1)}, bf16[256,128]{1,0:T(8,128)(2,1)S(1)}) custom-call(bf16[2,8192,128]{2,1,0:T(8,128)(2,1)S(1)} %copy-done, bf16[512,512]{1,0:T(8,128)(2,1)S(1)} %copy-done.2), custom_call_target="tpu_custom_call" | custom-call | tf_op jit(solution)/shard_map/home/pallas_call | solution.py:549
  126.9 0.8 copy.13
  127.7 0.6 copy.14
  128.3 0.6 copy.15
Async XLA Ops:
  0.6 1.0 copy-start.3
  1.7 1.0 copy-start.4
  2.7 1.0 copy-start.5
  3.8 0.8 copy-start.8
  4.6 0.8 copy-start.9
  27.9 1.9 %copy-start.1 = (bf16[2,8192,128]{2,1,0:T(8,128)(2,1)}, bf16[2,8192,128]{2,1,0:T(8,128)(2,1)S(1)}, u32[]{:S(2)}) copy-start(bf16[2,8192,128]{2,1,0:T(8,128)(2,1)S(1)} %get-tuple-element.12.kv_ref) | copy-start | bytes 12582916
  29.9 0.8 copy-start.6
  30.7 0.8 copy-start.7
  31.5 0.6 copy-start.10
  64.8 2.2 %copy-start = (bf16[2,8192,128]{2,1,0:T(8,128)(2,1)S(1)}, bf16[2,8192,128]{2,1,0:T(8,128)(2,1)}, u32[]{:S(2)}) copy-start(bf16[2,8192,128]{2,1,0:T(8,128)(2,1)} %get-tuple-element.13.dkv_ref) | copy-start | bytes 12582916
  67.0 1.0 copy-start.2

commit v2 on v1

--- a/solution.py
+++ b/solution.py
@@ -259,11 +259,12 @@
 
 def grad_kernel(parents_ref, seg_ref, q_ref, do_ref, dg_ref, kv_ref,
                 dkv_ref, dq_ref,
-                acc, expd, keys, values, qr, dor, tops, listed):
+                acc, expd, keys, values, qr, dor, qt, dot_, tops, listed):
     place = Place()
     column = place.x * 4 + place.z
     n0 = jnp.sum((seg_ref[...] == 0).astype(jnp.int32))
     factor = SCALE * LOG2E
+    PIECE = 256
 
     acc[...] = jnp.zeros_like(acc)
 
@@ -290,8 +291,11 @@
         q_rows = q_ref[pl.ds(row, BLOCK), :]
         do_rows = do_ref[pl.ds(row, BLOCK), :]
         for h in range(4):
-            qr[h * D:(h + 1) * D, :] = q_rows[:, h * D:(h + 1) * D]
-            dor[h * D:(h + 1) * D, :] = do_rows[:, h * D:(h + 1) * D]
+            cols = slice(h * D, (h + 1) * D)
+            qr[cols, :] = q_rows[:, cols]
+            dor[cols, :] = do_rows[:, cols]
+            qt[:, cols] = q_rows[:, cols].T
+            dot_[:, cols] = do_rows[:, cols].T
         source = ((qb % 2) * 2 + qb // 2) * 2
         pair = dg_ref[source] + dg_ref[source + 1]
         out_dot = jnp.concatenate([pair[h:h + 1, :] for h in range(4)], axis=1)
@@ -300,59 +304,103 @@
         least = jnp.where(query_at >= n0, n0, 0)
         edge = jnp.where(q_start + BLOCK - 1 >= n0, n0, 0)
 
-        def scores_turn(g, state):
-            top, total = state
+        def fetch(g):
             base = pl.multiple_of(g * GROUP * BLOCK, GROUP * BLOCK)
-            at = pl.ds(base, GROUP * BLOCK)
-            masked = (g == 0) | (g * GROUP + GROUP > count)
             for i in range(GROUP):
                 b = listed[g * GROUP + i]
-                masked = masked | (b * BLOCK < edge)
                 rows = pl.ds(pl.multiple_of(b * BLOCK, BLOCK), BLOCK)
                 dest = pl.ds(pl.multiple_of(base + i * BLOCK, BLOCK), BLOCK)
                 keys[dest, :] = kv_ref[0, rows, :]
                 values[dest, :] = kv_ref[1, rows, :]
-            expd[at, :] = lax.dot_general(keys[at, :], qr[...], NT, preferred_element_type=F32)
-
-            @pl.when(masked)
-            def _():
-                for i in range(GROUP):
-                    b = listed[g * GROUP + i]
-                    start = jnp.where(g * GROUP + i < count, b * BLOCK, 2 * TOKENS)
-                    dest = pl.ds(pl.multiple_of(base + i * BLOCK, BLOCK), BLOCK)
-                    key_at = start + lax.broadcasted_iota(jnp.int32, (BLOCK, ROWS), 0)
-                    ok = (key_at <= query_at) & (key_at >= least)
-                    expd[dest, :] = jnp.where(ok, expd[dest, :], NEG)
-
-            scores = expd[at, :]
-            new_top = jnp.maximum(top, jnp.max(scores, axis=0, keepdims=True))
-            e = jnp.exp2((scores - new_top) * factor)
+
+        def scores_of(g, i, masked):
+            at = pl.ds(pl.multiple_of((g * GROUP + i) * BLOCK, BLOCK), BLOCK)
+            scores = lax.dot_general(kv_ref[0, pl.ds(pl.multiple_of(listed[g * GROUP + i] * BLOCK, BLOCK), BLOCK), :], qr[...], NT, preferred_element_type=F32)
+            if masked:
+                start = jnp.where(g * GROUP + i < count, listed[g * GROUP + i] * BLOCK, 2 * TOKENS)
+                key_at = start + lax.broadcasted_iota(jnp.int32, (BLOCK, ROWS), 0)
+                ok = (key_at <= query_at) & (key_at >= least)
+                scores = jnp.where(ok, scores, NEG)
+            return at, scores
+
+        def fold(e):
+            return jnp.sum(e.reshape(BLOCK // 8, 8, ROWS), axis=0)
+
+        def fast_turn(masked, top, g, total):
+            fetch(g)
+            for i in range(GROUP):
+                at, scores = scores_of(g, i, masked)
+                e = jnp.exp2((scores - top) * factor)
+                expd[at, :] = e
+                total = total + fold(e)
+            return total
+
+        def slow_turn(g, state):
+            top, total = state
+            for i in range(GROUP):
+                at, scores = scores_of(g, i, True)
+                new_top = jnp.maximum(top, jnp.max(scores, axis=0, keepdims=True))
+                e = jnp.exp2((scores - new_top) * factor)
+                expd[at, :] = e
+                tops[pl.ds(pl.multiple_of((g * GROUP + i) * 8, 8), 8), :] = jnp.broadcast_to(new_top, (8, ROWS))
+                total = total * jnp.exp2((top - new_top) * factor) + jnp.sum(e, axis=0, keepdims=True)
+                top = new_top
+            return (top, total)
+
+        fetch(0)
+        firsts = [scores_of(0, i, True) for i in range(GROUP)]
+        top = functools.reduce(jnp.maximum, [jnp.max(f[1], axis=0, keepdims=True) for f in firsts])
+        total = jnp.zeros((8, ROWS), F32)
+        for at, scores in firsts:
+            e = jnp.exp2((scores - top) * factor)
             expd[at, :] = e
-            tops[g] = jnp.broadcast_to(new_top, (8, ROWS))
-            total = total * jnp.exp2((top - new_top) * factor) + jnp.sum(e, axis=0, keepdims=True)
-            return (new_top, total)
-
-        top, total = lax.fori_loop(
-            0, groups, scores_turn,
-            (jnp.full((1, ROWS), NEG, F32), jnp.zeros((1, ROWS), F32)))
-        inverse = 1.0 / total
+            total = total + fold(e)
+
+        def clear(g, n):
+            last = listed[jnp.minimum(g * GROUP + GROUP, count) - 1]
+            return jnp.where((g * GROUP + GROUP <= count) & (last * BLOCK >= edge), g + 1, n)
+
+        plain = lax.fori_loop(1, groups, clear, jnp.int32(1))
+        total = lax.fori_loop(1, plain, functools.partial(fast_turn, False, top), total)
+        total = lax.fori_loop(plain, groups, functools.partial(fast_turn, True, top), total)
+        total = jnp.sum(total, axis=0, keepdims=True)
+        tops[0:8, :] = jnp.broadcast_to(1.0 / total, (8, ROWS))
+        safe = jnp.max(total) < 1e30
+
+        @pl.when(jnp.logical_not(safe))
+        def _():
+            state = (jnp.full((1, ROWS), NEG, F32), jnp.zeros((1, ROWS), F32))
+            top, total = lax.fori_loop(0, groups, slow_turn, state)
+            inverse = 1.0 / total
+
+            def rescale(n, c):
+                at = pl.ds(pl.multiple_of(n * BLOCK, BLOCK), BLOCK)
+                share = jnp.exp2((tops[pl.ds(pl.multiple_of(n * 8, 8), 8), :][0:1] - top) * factor) * inverse
+                expd[at, :] = expd[at, :] * share
+                return c
+
+            lax.fori_loop(0, groups * GROUP, rescale, 0)
+            tops[0:8, :] = jnp.ones((8, ROWS), F32)
+
+        inverse = tops[0:1, :]
 
         def grad_turn(g, dqt):
-            base = pl.multiple_of(g * GROUP * BLOCK, GROUP * BLOCK)
-            at = pl.ds(base, GROUP * BLOCK)
-            share = jnp.exp2((tops[g][0:1, :] - top) * factor) * inverse
-            weights = expd[at, :] * share
-            half = weights.astype(BF16)
-            weight_grad = lax.dot_general(values[at, :], dor[...], NT, preferred_element_type=F32)
-            score_grad = (weights * (weight_grad - out_dot)).astype(BF16)
-            dv = jnp.dot(half, dor[...], preferred_element_type=F32)
-            dk = jnp.dot(score_grad, qr[...], preferred_element_type=F32)
-            for i in range(GROUP):
-                b = listed[g * GROUP + i]
-                rows = pl.ds(pl.multiple_of(b * BLOCK, BLOCK), BLOCK)
-                acc[0, rows, :] += dk[i * BLOCK:(i + 1) * BLOCK, :]
-                acc[1, rows, :] += dv[i * BLOCK:(i + 1) * BLOCK, :]
-            return dqt + lax.dot_general(keys[at, :], score_grad, TN, preferred_element_type=F32)
+            for i in range(GROUP * BLOCK // PIECE):
+                base = pl.multiple_of(g * GROUP * BLOCK + i * PIECE, PIECE)
+                at = pl.ds(base, PIECE)
+                weights = expd[at, :] * inverse
+                half = weights.astype(BF16)
+                weight_grad = lax.dot_general(values[at, :], dor[...], NT, preferred_element_type=F32)
+                score_grad = (weights * (weight_grad - out_dot)).astype(BF16)
+                dv = jnp.dot(half, dor[...], preferred_element_type=F32)
+                dk = jnp.dot(score_grad, qr[...], preferred_element_type=F32)
+                for n in range(PIECE // BLOCK):
+                    b = listed[g * GROUP + i * (PIECE // BLOCK) + n]
+                    rows = pl.ds(pl.multiple_of(b * BLOCK, BLOCK), BLOCK)
+                    acc[0, rows, :] += dk[n * BLOCK:(n + 1) * BLOCK, :]
+                    acc[1, rows, :] += dv[n * BLOCK:(n + 1) * BLOCK, :]
+                dqt = dqt + lax.dot_general(keys[at, :], score_grad, TN, preferred_element_type=F32)
+            return dqt
 
         dqt = lax.fori_loop(0, groups, grad_turn, jnp.zeros((D, ROWS), F32))
         for h in range(4):
@@ -519,7 +567,7 @@
             DMA((2,)), DMA((2,)), DMA((32,)), DMA((16,)), DMA((16,)),
         ],
         compiler_params=pltpu.CompilerParams(
-            collective_id=0, has_side_effects=True, vmem_limit_bytes=16 * MIB),
+            collective_id=0, has_side_effects=True, vmem_limit_bytes=60 * MIB),
         name="spread",
     )(q, do, o, k, v)
 
@@ -537,10 +585,12 @@
             pltpu.VMEM((48 * BLOCK, D), BF16),
             pltpu.VMEM((ROWS, D), BF16),
             pltpu.VMEM((ROWS, D), BF16),
-            pltpu.VMEM((12, 8, ROWS), F32),
+            pltpu.VMEM((D, ROWS), BF16),
+            pltpu.VMEM((D, ROWS), BF16),
+            pltpu.VMEM((48 * 8, ROWS), F32),
             pltpu.SMEM((64,), jnp.int32),
         ],
-        compiler_params=pltpu.CompilerParams(vmem_limit_bytes=56 * MIB),
+        compiler_params=pltpu.CompilerParams(vmem_limit_bytes=60 * MIB),
         name="grads",
     )(parents, seg, q, do, dg, kv)
 
@@ -566,7 +616,7 @@
             DMA((12,)), DMA((2,)), DMA((3,)), DMA((3, 3)), DMA((2,)), DMA((2,)), DMA((2,)),
         ],
         compiler_params=pltpu.CompilerParams(
-            collective_id=1, has_side_effects=True, vmem_limit_bytes=32 * MIB),
+            collective_id=1, has_side_effects=True, vmem_limit_bytes=60 * MIB),
         name="home",
     )(dkv, dq)
 

time: 129 us -> 107 us (0.83)
  Pallas kernels: 114 us -> 101 us
  local copies, waits for them, and re-layouts: 14.3 us -> 4.81 us
    pallas_call x1, Pallas kernels: 58.9 us -> 47.5 us  [home(): pl.pallas_call(home_kernel, out_shape=(struct((64, 4096), BF16), struct((...]
    unnamed x25 -> x3, local copies, waits for them, and re-layouts: 14.3 us -> 4.81 us
    pallas_call x1, Pallas kernels: 32.7 us -> 28.3 us  [grads(): pl.pallas_call(grad_kernel, out_shape=(struct((2, TOKENS, D), BF16), stru...]
    pallas_call x1, Pallas kernels: 22.5 us -> 24.8 us  [spread(): pl.pallas_call(spread_kernel, out_shape=(struct((COLUMN, ROWS), BF16), st...]
where the time goes in v2:
time: 107 us; the launch traced here: 106 us
  Pallas kernels  101 us (94%)
  local copies, waits for them, and re-layouts  4.81 us (4%)
    pallas_call x1, Pallas kernels, home(): pl.pallas_call(home_kernel, out_shape=(struct((64, 4096), BF16), struct((...  47.5 us
    pallas_call x1, Pallas kernels, grads(): pl.pallas_call(grad_kernel, out_shape=(struct((2, TOKENS, D), BF16), stru...  28.3 us
    pallas_call x1, Pallas kernels, spread(): pl.pallas_call(spread_kernel, out_shape=(struct((COLUMN, ROWS), BF16), st...  24.8 us
    unnamed x3, local copies, waits for them, and re-layouts  4.81 us

profile of v2, /device:TPU:10, one launch (start us, length us, event | category | flops | bytes accessed | tf_op | source)
XLA Modules:
  0.0 106.1 jit_solution(2095177230454589063)
XLA Ops:
  0.6 24.8 %spread.1 = (bf16[512,512]{1,0:T(8,128)(2,1)}, bf16[512,512]{1,0:T(8,128)(2,1)}, f32[8,8,128]{2,1,0:T(8,128)}, bf16[2,8192,128]{2,1,0:T(8,128)(2,1)}) custom-call(bf16[64,4096]{1,0:T(8,128)(2,1)} %q_ref.1, bf16[64,4096]{1,0:T(8,128)(2,1)} %do_ref.1, bf16[64,4096]{1,0:T(8,128)(2,1)} %o_ref.1, bf16[256,128]{1,0:T(8,128)(2,1)} %k_ref.1, bf16[256,128]{1,0:T(8,128)(2,1)} %v_ref.1), custom_call_target="tpu_custom_call" | custom-call | tf_op jit(solution)/shard_map/spread/pallas_call | solution.py:558
  25.5 28.3 %grads.1 = (bf16[2,8192,128]{2,1,0:T(8,128)(2,1)}, bf16[512,512]{1,0:T(8,128)(2,1)}) custom-call(s32[64]{0:T(128)} %parents_ref.1, s32[64,128]{1,0:T(8,128)} %bitcast.1, bf16[512,512]{1,0:T(8,128)(2,1)} %get-tuple-element.9.q_ref, bf16[512,512]{1,0:T(8,128)(2,1)} %get-tuple-element.10.do_ref, f32[8,8,128]{2,1,0:T(8,128)} %get-tuple-element.11.dg_ref, ...), custom_call_target="tpu_custom_call" | custom-call | tf_op jit(solution)/shard_map/grads/pallas_call | solution.py:576
  53.8 47.5 %home.1 = (bf16[64,4096]{1,0:T(8,128)(2,1)}, bf16[256,128]{1,0:T(8,128)(2,1)}, bf16[256,128]{1,0:T(8,128)(2,1)}) custom-call(bf16[2,8192,128]{2,1,0:T(8,128)(2,1)} %get-tuple-element.13.dkv_ref, bf16[512,512]{1,0:T(8,128)(2,1)} %get-tuple-element.14.dq_ref), custom_call_target="tpu_custom_call" | custom-call | tf_op jit(solution)/shard_map/home/pallas_call | solution.py:599
  101.3 1.9 %copy.13 = bf16[64,4096]{1,0:T(8,128)(2,1)} copy(bf16[64,4096]{1,0:T(8,128)(2,1)} %get-tuple-element.18) | data formatting | bytes 1048576
  103.2 1.5 %copy.14 = bf16[256,128]{1,0:T(8,128)(2,1)} copy(bf16[256,128]{1,0:T(8,128)(2,1)} %get-tuple-element.19) | data formatting | bytes 131072
  104.7 1.5 %copy.15 = bf16[256,128]{1,0:T(8,128)(2,1)} copy(bf16[256,128]{1,0:T(8,128)(2,1)} %get-tuple-element.20) | data formatting | bytes 131072

commit v3 on v1

--- a/solution.py
+++ b/solution.py
@@ -15,6 +15,9 @@
 SECTION = 2048
 NEAR = 3
 GROUP = 4
+SCORES_AT_ONCE = 4
+GRADS_AT_ONCE = 2
+SLOTS = 30
 ROWS = 512
 SCALE = 1.0 / math.sqrt(D)
 LOG2E = math.log2(math.e)
@@ -257,20 +260,43 @@
         pl.when(away)(copy.wait_send)
 
 
-def grad_kernel(parents_ref, seg_ref, q_ref, do_ref, dg_ref, kv_ref,
-                dkv_ref, dq_ref,
-                acc, expd, keys, values, qr, dor, tops, listed):
+def grad_kernel(parents_ref, seg_ref, q_hbm, do_hbm, dg_ref, kv_hbm,
+                dkv_hbm, dq_ref,
+                acc, expd, kv, stage, q_all, do_all, qr, dor, tops, cuts, inv, dqt,
+                chain, in_sem, kv_sem, out_sem):
     place = Place()
-    column = place.x * 4 + place.z
+    x = place.x
+    column = x * 4 + place.z
+    first_block = (x - (NEAR - 1)) * (SECTION // BLOCK)
+    factor = SCALE * LOG2E
+
+    loads = []
+    for slot in (2, 1, 0):
+        d = 2 - slot
+        rows = pl.ds(pl.multiple_of(((x + 4 - d) % 4) * SECTION, SECTION), SECTION)
+        for p in range(2):
+            copy = pltpu.make_async_copy(
+                kv_hbm.at[p, rows, :], kv.at[p, pl.ds(slot * SECTION, SECTION), :],
+                kv_sem.at[p, slot])
+            pl.when(x >= d)(copy.start)
+            loads.append((x >= d, copy))
+    q_copy = pltpu.make_async_copy(q_hbm, q_all, in_sem.at[0])
+    do_copy = pltpu.make_async_copy(do_hbm, do_all, in_sem.at[1])
+    q_copy.start()
+    do_copy.start()
+
     n0 = jnp.sum((seg_ref[...] == 0).astype(jnp.int32))
-    factor = SCALE * LOG2E
-
-    acc[...] = jnp.zeros_like(acc)
-
-    def one_block(qb, carry):
+
+    chains = [None] * 4
+    free = jnp.int32(0)
+    for qb in (3, 2, 1, 0):
         gb = column * 4 + qb
-        q_start = gb * BLOCK
-        lowest = jnp.where(q_start >= n0, n0, 0)
+        lowest = jnp.where(gb * BLOCK >= n0, n0, 0)
+        if qb == 3:
+            shared = jnp.bool_(False)
+        else:
+            base, count, low = chains[qb + 1]
+            shared = (parents_ref[gb + 1] == gb) & (low == lowest)
 
         def more(state):
             b, n = state
@@ -278,91 +304,215 @@
 
         def note(state):
             b, n = state
-            listed[n] = b
+            chain[n] = b
             return (parents_ref[b], n + 1)
 
-        _, count = lax.while_loop(more, note, (gb, jnp.int32(0)))
-        for i in range(GROUP - 1):
-            listed[count + i] = gb
-        groups = (count + GROUP - 1) // GROUP
-
-        row = pl.multiple_of(qb * BLOCK, BLOCK)
-        q_rows = q_ref[pl.ds(row, BLOCK), :]
-        do_rows = do_ref[pl.ds(row, BLOCK), :]
+        _, stop = lax.while_loop(more, note, (jnp.where(shared, -1, gb), free))
+        own = (free, stop - free, lowest)
+        if qb < 3:
+            own = (jnp.where(shared, base + 1, free), jnp.where(shared, count - 1, stop - free), lowest)
+        chains[qb] = own
+        free = stop
+
+    for slot in range(NEAR):
+        @pl.when(x >= 2 - slot)
+        def _():
+            for p in range(2):
+                acc[p, slot * SECTION:(slot + 1) * SECTION, :] = jnp.zeros((SECTION, D), F32)
+    dqt[...] = jnp.zeros_like(dqt)
+
+    q_copy.wait()
+    do_copy.wait()
+    for qb in range(4):
         for h in range(4):
-            qr[h * D:(h + 1) * D, :] = q_rows[:, h * D:(h + 1) * D]
-            dor[h * D:(h + 1) * D, :] = do_rows[:, h * D:(h + 1) * D]
-        source = ((qb % 2) * 2 + qb // 2) * 2
-        pair = dg_ref[source] + dg_ref[source + 1]
-        out_dot = jnp.concatenate([pair[h:h + 1, :] for h in range(4)], axis=1)
-
-        query_at = q_start + lax.broadcasted_iota(jnp.int32, (1, ROWS), 1) % BLOCK
-        least = jnp.where(query_at >= n0, n0, 0)
-        edge = jnp.where(q_start + BLOCK - 1 >= n0, n0, 0)
-
-        def scores_turn(g, state):
-            top, total = state
-            base = pl.multiple_of(g * GROUP * BLOCK, GROUP * BLOCK)
-            at = pl.ds(base, GROUP * BLOCK)
-            masked = (g == 0) | (g * GROUP + GROUP > count)
+            rows, cols = slice(qb * BLOCK, (qb + 1) * BLOCK), slice(h * D, (h + 1) * D)
+            qr[qb * ROWS + h * D:qb * ROWS + (h + 1) * D, :] = q_all[rows, cols]
+            dor[qb * ROWS + h * D:qb * ROWS + (h + 1) * D, :] = do_all[rows, cols]
+    for cond, copy in loads:
+        pl.when(cond)(copy.wait)
+
+    def block_rows(b):
+        return pl.ds(pl.multiple_of((b - first_block) * BLOCK, BLOCK), BLOCK)
+
+    def gathered(p, blocks):
+        return jnp.concatenate([kv[p, block_rows(b), :] for b in blocks], axis=0)
+
+    def row_of(q):
+        return pl.ds(pl.multiple_of(q * 8, 8), 1)
+
+    def lines_of(q):
+        return pl.ds(pl.multiple_of(q * 8, 8), 8)
+
+    def rows_of(qb):
+        return pl.ds(pl.multiple_of(qb * ROWS, ROWS), ROWS)
+
+    def fold(e):
+        return jnp.sum(e.reshape(-1, 8, ROWS), axis=0)
+
+    def one_half(half, carry):
+        def pick(even, odd):
+            return jnp.where(half == 0, even, odd)
+
+        bases = [pick(chains[q][0], chains[q + 2][0]) for q in range(2)]
+        counts = [pick(chains[q][1], chains[q + 2][1]) for q in range(2)]
+        lows = [pick(chains[q][2], chains[q + 2][2]) for q in range(2)]
+        starts = [(column * 4 + half * 2 + q) * BLOCK for q in range(2)]
+        steps = [(counts[q] + GROUP - 1) // GROUP - 1 for q in range(2)]
+        items = steps[0] + steps[1]
+
+        def blocks_of(q, g):
+            base = jnp.where(q == 0, bases[0], bases[1])
+            count = jnp.where(q == 0, counts[0], counts[1])
+            diagonal = column * 4 + half * 2 + q
+            blocks, real = [], []
             for i in range(GROUP):
-                b = listed[g * GROUP + i]
-                masked = masked | (b * BLOCK < edge)
-                rows = pl.ds(pl.multiple_of(b * BLOCK, BLOCK), BLOCK)
-                dest = pl.ds(pl.multiple_of(base + i * BLOCK, BLOCK), BLOCK)
-                keys[dest, :] = kv_ref[0, rows, :]
-                values[dest, :] = kv_ref[1, rows, :]
-            expd[at, :] = lax.dot_general(keys[at, :], qr[...], NT, preferred_element_type=F32)
-
-            @pl.when(masked)
+                at = g * GROUP + i
+                here = at < count
+                index = base + jnp.where(at == 0, 0, jnp.where(at == 1, count - 1, at - 1))
+                blocks.append(jnp.where(here, chain[jnp.where(here, index, 0)], diagonal))
+                real.append(here)
+            return blocks, real
+
+        def item(slot):
+            t = slot - 2
+            late = t >= steps[0]
+            q = jnp.where(slot < 2, slot, late.astype(jnp.int32))
+            g = jnp.where(slot < 2, 0, t - jnp.where(late, steps[0], 0) + 1)
+            return q, g
+
+        def expd_rows(slot, i=0, n=GROUP):
+            return pl.ds(pl.multiple_of(slot * GROUP * BLOCK + i * BLOCK, BLOCK), n * BLOCK)
+
+        def masked_scores(q, g):
+            blocks, real = blocks_of(q, g)
+            start = (column * 4 + half * 2 + q) * BLOCK
+            query_at = start + lax.broadcasted_iota(jnp.int32, (1, ROWS), 1) % BLOCK
+            least = jnp.where(query_at >= n0, n0, 0)
+            scores = lax.dot_general(gathered(0, blocks), qr[rows_of(half * 2 + q), :], NT,
+                                     preferred_element_type=F32)
+            parts = []
+            for i in range(GROUP):
+                first = jnp.where(real[i], blocks[i] * BLOCK, 2 * TOKENS)
+                key_at = first + lax.broadcasted_iota(jnp.int32, (BLOCK, ROWS), 0)
+                ok = (key_at <= query_at) & (key_at >= least)
+                parts.append(jnp.where(ok, scores[i * BLOCK:(i + 1) * BLOCK, :], NEG))
+            return jnp.concatenate(parts, axis=0)
+
+        for q in range(2):
+            scores = masked_scores(q, 0)
+            top = jnp.max(scores, axis=0, keepdims=True)
+            e = jnp.exp2((scores - top) * factor)
+            expd[expd_rows(q), :] = e
+            inv[lines_of(q), :] = fold(e)
+            query_at = starts[q] + lax.broadcasted_iota(jnp.int32, (1, ROWS), 1) % BLOCK
+            cut = jnp.where((query_at >= n0) & (starts[q] < n0), -NEG, 0.0)
+            cuts[lines_of(q), :] = jnp.broadcast_to(top + cut, (8, ROWS))
+
+        def scores_turn(n, c):
+            for u in range(SCORES_AT_ONCE):
+                slot = 2 + n * SCORES_AT_ONCE + u
+                q, g = item(slot)
+                blocks, real = blocks_of(q, g)
+                scores = lax.dot_general(gathered(0, blocks), qr[rows_of(half * 2 + q), :], NT,
+                                         preferred_element_type=F32)
+                top = cuts[row_of(q), :]
+                sums = None
+                for i in range(GROUP):
+                    away = top + jnp.where(real[i], 0.0, -NEG)
+                    e = jnp.exp2((scores[i * BLOCK:(i + 1) * BLOCK, :] - away) * factor)
+                    expd[expd_rows(slot, i, 1), :] = e
+                    sums = fold(e) if sums is None else sums + fold(e)
+                inv[lines_of(q), :] += sums
+            return c
+
+        lax.fori_loop(0, (items + SCORES_AT_ONCE - 1) // SCORES_AT_ONCE, scores_turn, 0)
+        totals = [jnp.sum(inv[q * 8:(q + 1) * 8, :], axis=0, keepdims=True) for q in range(2)]
+        safe = jnp.max(jnp.maximum(totals[0], totals[1])) < 1e30
+        for q in range(2):
+            inv[q * 8:(q + 1) * 8, :] = jnp.broadcast_to(1.0 / totals[q], (8, ROWS))
+
+        @pl.when(jnp.logical_not(safe))
+        def _():
+            cuts[...] = jnp.full_like(cuts, NEG)
+            inv[...] = jnp.zeros_like(inv)
+
+            def again(slot, c):
+                q, g = item(slot)
+                scores = masked_scores(q, g)
+                top, total = cuts[row_of(q), :], inv[row_of(q), :]
+                new_top = jnp.maximum(top, jnp.max(scores, axis=0, keepdims=True))
+                e = jnp.exp2((scores - new_top) * factor)
+                expd[expd_rows(slot), :] = e
+                total = total * jnp.exp2((top - new_top) * factor) + jnp.sum(
+                    e, axis=0, keepdims=True)
+                cuts[lines_of(q), :] = jnp.broadcast_to(new_top, (8, ROWS))
+                tops[lines_of(slot), :] = jnp.broadcast_to(new_top, (8, ROWS))
+                inv[lines_of(q), :] = jnp.broadcast_to(total, (8, ROWS))
+                return c
+
+            def settle(slot, c):
+                q, g = item(slot)
+                share = jnp.exp2((tops[row_of(slot), :] - cuts[row_of(q), :]) * factor)
+                expd[expd_rows(slot), :] = expd[expd_rows(slot), :] * (share / inv[row_of(q), :])
+                return c
+
+            lax.fori_loop(0, items + 2, again, 0)
+            lax.fori_loop(0, items + 2, settle, 0)
+            inv[...] = jnp.ones_like(inv)
+
+        def grads_turn(n, c):
+            work = []
+            for u in range(GRADS_AT_ONCE):
+                slot = n * GRADS_AT_ONCE + u
+                q, g = item(slot)
+                blocks, _ = blocks_of(q, g)
+                do_rows = dor[rows_of(half * 2 + q), :]
+                weight_grad = lax.dot_general(gathered(1, blocks), do_rows, NT,
+                                              preferred_element_type=F32)
+                work.append((slot, q, blocks, do_rows, weight_grad))
+            for slot, q, blocks, do_rows, weight_grad in work:
+                qb = half * 2 + q
+                source = ((qb % 2) * 2 + qb // 2) * 2
+                pair = dg_ref[source] + dg_ref[source + 1]
+                out_dot = jnp.concatenate([pair[h:h + 1, :] for h in range(4)], axis=1)
+                weights = expd[expd_rows(slot), :] * inv[row_of(q), :]
+                halved = weights.astype(BF16)
+                score_grad = (weights * (weight_grad - out_dot)).astype(BF16)
+                dv = jnp.dot(halved, do_rows, preferred_element_type=F32)
+                dk = jnp.dot(score_grad, qr[rows_of(qb), :], preferred_element_type=F32)
+                into = pl.ds(pl.multiple_of(qb * D, D), D)
+                dqt[into, :] += lax.dot_general(gathered(0, blocks), score_grad, TN,
+                                                preferred_element_type=F32)
+                for i, b in enumerate(blocks):
+                    rows = block_rows(b)
+                    acc[0, rows, :] += dk[i * BLOCK:(i + 1) * BLOCK, :]
+                    acc[1, rows, :] += dv[i * BLOCK:(i + 1) * BLOCK, :]
+            return c
+
+        lax.fori_loop(0, (items + 2 + GRADS_AT_ONCE - 1) // GRADS_AT_ONCE, grads_turn, 0)
+        return carry
+
+    lax.fori_loop(0, 2, one_half, 0)
+
+    stores = []
+    for slot in range(NEAR):
+        for p, by in ((0, SCALE), (1, 1.0)):
+            at = slice(slot * SECTION, (slot + 1) * SECTION)
+            copy = pltpu.make_async_copy(
+                stage.at[p, pl.ds(slot * SECTION, SECTION), :], dkv_hbm.at[p, slot],
+                out_sem.at[p, slot])
+
+            @pl.when(x >= 2 - slot)
             def _():
-                for i in range(GROUP):
-                    b = listed[g * GROUP + i]
-                    start = jnp.where(g * GROUP + i < count, b * BLOCK, 2 * TOKENS)
-                    dest = pl.ds(pl.multiple_of(base + i * BLOCK, BLOCK), BLOCK)
-                    key_at = start + lax.broadcasted_iota(jnp.int32, (BLOCK, ROWS), 0)
-                    ok = (key_at <= query_at) & (key_at >= least)
-                    expd[dest, :] = jnp.where(ok, expd[dest, :], NEG)
-
-            scores = expd[at, :]
-            new_top = jnp.maximum(top, jnp.max(scores, axis=0, keepdims=True))
-            e = jnp.exp2((scores - new_top) * factor)
-            expd[at, :] = e
-            tops[g] = jnp.broadcast_to(new_top, (8, ROWS))
-            total = total * jnp.exp2((top - new_top) * factor) + jnp.sum(e, axis=0, keepdims=True)
-            return (new_top, total)
-
-        top, total = lax.fori_loop(
-            0, groups, scores_turn,
-            (jnp.full((1, ROWS), NEG, F32), jnp.zeros((1, ROWS), F32)))
-        inverse = 1.0 / total
-
-        def grad_turn(g, dqt):
-            base = pl.multiple_of(g * GROUP * BLOCK, GROUP * BLOCK)
-            at = pl.ds(base, GROUP * BLOCK)
-            share = jnp.exp2((tops[g][0:1, :] - top) * factor) * inverse
-            weights = expd[at, :] * share
-            half = weights.astype(BF16)
-            weight_grad = lax.dot_general(values[at, :], dor[...], NT, preferred_element_type=F32)
-            score_grad = (weights * (weight_grad - out_dot)).astype(BF16)
-            dv = jnp.dot(half, dor[...], preferred_element_type=F32)
-            dk = jnp.dot(score_grad, qr[...], preferred_element_type=F32)
-            for i in range(GROUP):
-                b = listed[g * GROUP + i]
-                rows = pl.ds(pl.multiple_of(b * BLOCK, BLOCK), BLOCK)
-                acc[0, rows, :] += dk[i * BLOCK:(i + 1) * BLOCK, :]
-                acc[1, rows, :] += dv[i * BLOCK:(i + 1) * BLOCK, :]
-            return dqt + lax.dot_general(keys[at, :], score_grad, TN, preferred_element_type=F32)
-
-        dqt = lax.fori_loop(0, groups, grad_turn, jnp.zeros((D, ROWS), F32))
+                stage[p, at, :] = (acc[p, at, :] * by).astype(BF16)
+                copy.start()
+            stores.append((x >= 2 - slot, copy))
+    for qb in range(4):
         for h in range(4):
-            part = dqt[:, h * D:(h + 1) * D].T * SCALE
-            dq_ref[pl.ds(row, BLOCK), h * D:(h + 1) * D] = part.astype(BF16)
-        return carry
-
-    lax.fori_loop(0, 4, one_block, 0)
-    dkv_ref[0] = (acc[0] * SCALE).astype(BF16)
-    dkv_ref[1] = acc[1].astype(BF16)
+            part = dqt[qb * D:(qb + 1) * D, h * D:(h + 1) * D].T * SCALE
+            dq_ref[qb * BLOCK:(qb + 1) * BLOCK, h * D:(h + 1) * D] = part.astype(BF16)
+    for cond, copy in stores:
+        pl.when(cond)(copy.wait)
 
 
 def home_kernel(dkv_ref, dq_ref,
@@ -376,8 +526,7 @@
     sibling = place.at(core=1 - core)
 
     def section(p, d):
-        start = pl.multiple_of(((x + 4 - d) % 4) * SECTION, SECTION)
-        return dkv_ref.at[p, pl.ds(start, SECTION), :]
+        return dkv_ref.at[p, 2 - d]
 
     sib_copies = []
     own_copies = []
@@ -519,7 +668,7 @@
             DMA((2,)), DMA((2,)), DMA((32,)), DMA((16,)), DMA((16,)),
         ],
         compiler_params=pltpu.CompilerParams(
-            collective_id=0, has_side_effects=True, vmem_limit_bytes=16 * MIB),
+            collective_id=0, has_side_effects=True, vmem_limit_bytes=60 * MIB),
         name="spread",
     )(q, do, o, k, v)
 
@@ -527,20 +676,26 @@
 def grads(parents, seg, q, do, dg, kv):
     return pl.pallas_call(
         grad_kernel,
-        out_shape=(struct((2, TOKENS, D), BF16), struct((COLUMN, ROWS), BF16)),
-        in_specs=[SMEM, VMEM, VMEM, VMEM, VMEM, VMEM],
-        out_specs=(VMEM, VMEM),
+        out_shape=(struct((2, NEAR, SECTION, D), BF16), struct((COLUMN, ROWS), BF16)),
+        in_specs=[SMEM, VMEM, ANY, ANY, VMEM, ANY],
+        out_specs=(ANY, VMEM),
         scratch_shapes=[
-            pltpu.VMEM((2, TOKENS, D), F32),
-            pltpu.VMEM((48 * BLOCK, ROWS), F32),
-            pltpu.VMEM((48 * BLOCK, D), BF16),
-            pltpu.VMEM((48 * BLOCK, D), BF16),
-            pltpu.VMEM((ROWS, D), BF16),
-            pltpu.VMEM((ROWS, D), BF16),
-            pltpu.VMEM((12, 8, ROWS), F32),
-            pltpu.SMEM((64,), jnp.int32),
+            pltpu.VMEM((2, NEAR * SECTION, D), F32),
+            pltpu.VMEM((SLOTS * GROUP * BLOCK, ROWS), F32),
+            pltpu.VMEM((2, NEAR * SECTION, D), BF16),
+            pltpu.VMEM((2, NEAR * SECTION, D), BF16),
+            pltpu.VMEM((COLUMN, ROWS), BF16),
+            pltpu.VMEM((COLUMN, ROWS), BF16),
+            pltpu.VMEM((4 * ROWS, D), BF16),
+            pltpu.VMEM((4 * ROWS, D), BF16),
+            pltpu.VMEM((SLOTS * 8, ROWS), F32),
+            pltpu.VMEM((16, ROWS), F32),
+            pltpu.VMEM((16, ROWS), F32),
+            pltpu.VMEM((4 * D, ROWS), F32),
+            pltpu.SMEM((256,), jnp.int32),
+            DMA((2,)), DMA((2, NEAR)), DMA((2, NEAR)),
         ],
-        compiler_params=pltpu.CompilerParams(vmem_limit_bytes=56 * MIB),
+        compiler_params=pltpu.CompilerParams(vmem_limit_bytes=60 * MIB),
         name="grads",
     )(parents, seg, q, do, dg, kv)
 
@@ -566,15 +721,41 @@
             DMA((12,)), DMA((2,)), DMA((3,)), DMA((3, 3)), DMA((2,)), DMA((2,)), DMA((2,)),
         ],
         compiler_params=pltpu.CompilerParams(
-            collective_id=1, has_side_effects=True, vmem_limit_bytes=32 * MIB),
+            collective_id=1, has_side_effects=True, vmem_limit_bytes=60 * MIB),
         name="home",
     )(dkv, dq)
+
+
+def hand_over_kernel(*refs):
+    copies = []
+    for n in range(3):
+        src, dst = refs[n], refs[3 + n]
+        rows = src.shape[0] // 4
+        for i in range(4):
+            at = pl.ds(i * rows, rows)
+            copies.append(pltpu.make_async_copy(src.at[at, :], dst.at[at, :], refs[6].at[n, i]))
+    for copy in copies:
+        copy.start()
+    for copy in copies:
+        copy.wait()
+
+
+def hand_over(*arrays):
+    return pl.pallas_call(
+        hand_over_kernel,
+        out_shape=tuple(struct(a.shape, a.dtype) for a in arrays),
+        in_specs=[ANY] * 3,
+        out_specs=(ANY,) * 3,
+        scratch_shapes=[DMA((3, 4))],
+        compiler_params=pltpu.CompilerParams(vmem_limit_bytes=60 * MIB),
+        name="hand_over",
+    )(*arrays)
 
 
 def local(query_rows, key_rows, value_rows, attn_output, out_grad, segments, parents):
     q, do, dg, kv = spread(query_rows, out_grad, attn_output, key_rows, value_rows)
     dkv, dq = grads(parents, segments.reshape(64, 128), q, do, dg, kv)
-    return home(dkv, dq)
+    return hand_over(*home(dkv, dq))
 
 
 def solution(mesh):

time: 129 us -> 115 us (0.89)
  local copies, waits for them, and re-layouts: 14.3 us -> 0 us
    unnamed x25 -> x0, local copies, waits for them, and re-layouts: 14.3 us -> none
    pallas_call x1, Pallas kernels: 58.9 us -> 44.8 us  [home(): pl.pallas_call(home_kernel, out_shape=(struct((64, 4096), BF16), struct((...]
    pallas_call x1 -> x2, Pallas kernels: 32.7 us -> 43.5 us  [the longest x1 22.4 us: grads(): pl.pallas_call(grad_kernel, out_shape=(struct((2, NEAR, SECTION, D), BF16...]
    pallas_call x1, Pallas kernels: 22.5 us -> 24.8 us  [spread(): pl.pallas_call(spread_kernel, out_shape=(struct((COLUMN, ROWS), BF16), st...]
where the time goes in v3:
time: 115 us; the launch traced here: 114 us
  Pallas kernels  113 us (98%)
    pallas_call x1, Pallas kernels, home(): pl.pallas_call(home_kernel, out_shape=(struct((64, 4096), BF16), struct((...  44.8 us
    pallas_call x1, Pallas kernels, spread(): pl.pallas_call(spread_kernel, out_shape=(struct((COLUMN, ROWS), BF16), st...  24.8 us
    pallas_call x1, Pallas kernels, grads(): pl.pallas_call(grad_kernel, out_shape=(struct((2, NEAR, SECTION, D), BF16...  22.4 us
    pallas_call x1, Pallas kernels, hand_over(): pl.pallas_call(hand_over_kernel, out_shape=tuple((struct(a.shape, a.dtype...  21.1 us

profile of v3, /device:TPU:10, one launch (start us, length us, event | category | flops | bytes accessed | tf_op | source)
XLA Modules:
  0.0 113.8 jit_solution(11319675504005692695)
XLA Ops:
  0.6 24.8 %spread.1 = (bf16[512,512]{1,0:T(8,128)(2,1)}, bf16[512,512]{1,0:T(8,128)(2,1)}, f32[8,8,128]{2,1,0:T(8,128)}, bf16[2,8192,128]{2,1,0:T(8,128)(2,1)}) custom-call(bf16[64,4096]{1,0:T(8,128)(2,1)} %q_ref.1, bf16[64,4096]{1,0:T(8,128)(2,1)} %do_ref.1, bf16[64,4096]{1,0:T(8,128)(2,1)} %o_ref.1, bf16[256,128]{1,0:T(8,128)(2,1)} %k_ref.1, bf16[256,128]{1,0:T(8,128)(2,1)} %v_ref.1), custom_call_target="tpu_custom_call" | custom-call | tf_op jit(solution)/shard_map/spread/pallas_call | solution.py:659
  25.5 22.4 %grads.1 = (bf16[2,3,2048,128]{3,2,1,0:T(8,128)(2,1)}, bf16[512,512]{1,0:T(8,128)(2,1)}) custom-call(s32[64]{0:T(128)} %parents_ref.1, s32[64,128]{1,0:T(8,128)} %bitcast.1, bf16[512,512]{1,0:T(8,128)(2,1)} %get-tuple-element.12.q_hbm, bf16[512,512]{1,0:T(8,128)(2,1)} %get-tuple-element.13.do_hbm, f32[8,8,128]{2,1,0:T(8,128)} %get-tuple-element.14.dg_ref, ...), custom_call_target="tpu_custom_call" | custom-call | tf_op jit(solution)/shard_map/grads/pallas_call | solution.py:677
  47.9 44.8 %home.1 = (bf16[64,4096]{1,0:T(8,128)(2,1)}, bf16[256,128]{1,0:T(8,128)(2,1)}, bf16[256,128]{1,0:T(8,128)(2,1)}) custom-call(bf16[2,3,2048,128]{3,2,1,0:T(8,128)(2,1)} %get-tuple-element.16.dkv_ref, bf16[512,512]{1,0:T(8,128)(2,1)} %get-tuple-element.17.dq_ref), custom_call_target="tpu_custom_call" | custom-call | tf_op jit(solution)/shard_map/home/pallas_call | solution.py:704
  92.7 21.1 %hand_over.1 = (bf16[64,4096]{1,0:T(8,128)(2,1)}, bf16[256,128]{1,0:T(8,128)(2,1)}, bf16[256,128]{1,0:T(8,128)(2,1)}) custom-call(bf16[64,4096]{1,0:T(8,128)(2,1)} %get-tuple-element.18.refs_0_, bf16[256,128]{1,0:T(8,128)(2,1)} %get-tuple-element.19.refs_1_, bf16[256,128]{1,0:T(8,128)(2,1)} %get-tuple-element.20.refs_2_), custom_call_target="tpu_custom_call" | custom-call | tf_op jit(solution)/shard_map/hand_over/pallas_call | solution.py:744

commit v4 on v3

--- a/solution.py
+++ b/solution.py
@@ -14,10 +14,11 @@
 COLUMN = 512
 SECTION = 2048
 NEAR = 3
+FAR_FIRST = (2, 1, 3, 0)
 GROUP = 4
 SCORES_AT_ONCE = 4
 GRADS_AT_ONCE = 2
-SLOTS = 30
+SLOTS = 26
 ROWS = 512
 SCALE = 1.0 / math.sqrt(D)
 LOG2E = math.log2(math.e)
@@ -102,12 +103,18 @@
                 pl.when(cond)(copy.wait_send)
 
 
-def spread_kernel(q_ref, do_ref, o_ref, k_ref, v_ref,
-                  qg_ref, dog_ref, dg_ref, kv_ref,
-                  dsrc, col_send, q_recv, do_recv, d_recv, local_sem,
+def spread_kernel(q_ref, do_ref, o_ref, k_ref, v_ref, seg_ref, parents_ref,
+                  qg_ref, dog_ref, dg_ref, kv_ref, seg_near, parents_near,
+                  do_near, o_near, near_sem, dsrc, col_send, q_recv, do_recv, d_recv, local_sem,
                   first_send, first_recv, piece_send, prim_recv, sib_recv):
     place = Place()
     x, z, core = place.x, place.z, place.core
+    nears = [pltpu.make_async_copy(do_ref, do_near, near_sem.at[0]),
+             pltpu.make_async_copy(o_ref, o_near, near_sem.at[1]),
+             pltpu.make_async_copy(seg_ref, seg_near, near_sem.at[2]),
+             pltpu.make_async_copy(parents_ref, parents_near, near_sem.at[3])]
+    for copy in nears:
+        copy.start()
     greet(place)
 
     first_row = pl.multiple_of((x * 4 + z) * COLUMN + place.ylo * 256, 256)
@@ -126,26 +133,31 @@
     my_row = pl.multiple_of(place.home_row(), 64)
     columns = Sends(col_send)
     locals_ = []
-    for t in range(8):
-        cols = pl.ds(t * ROWS, ROWS)
+    for away in (4, 5, 2, 3, 6, 7, 1, 0):
+        t = ((place.y + away // 2) % 4) * 2 + (core + away) % 2
+        cols = pl.ds(pl.multiple_of(t * ROWS, ROWS), ROWS)
         for n, (src, dst, recv) in enumerate(
                 ((q_ref, qg_ref, q_recv), (do_ref, dog_ref, do_recv))):
             target = dst.at[pl.ds(my_row, 64), :]
-            columns.start(place.own != t, src.at[:, cols], target, recv.at[place.own],
-                          place.in_column(t))
-            local = pltpu.make_async_copy(src.at[:, cols], target, local_sem.at[n])
-            pl.when(place.own == t)(local.start)
-            locals_.append((place.own == t, local))
+            if away:
+                columns.start(None, src.at[:, cols], target, recv.at[place.own],
+                              place.in_column(t))
+            else:
+                local = pltpu.make_async_copy(src.at[:, cols], target, local_sem.at[n])
+                local.start()
+                locals_.append((None, local))
 
     lane = lax.broadcasted_iota(jnp.int32, (8, 128), 1)
     line = lax.broadcasted_iota(jnp.int32, (8, 128), 0)
     mine = (lane // 64) == core
     ones = jnp.ones((8, D), BF16)
+    for copy in nears:
+        copy.wait()
     for t in range(8):
         tile = jnp.zeros((8, 128), F32)
         for r in range(4):
             cols = slice((t * 4 + r) * D, (t * 4 + r + 1) * D)
-            prod = do_ref[:, cols].astype(F32) * o_ref[:, cols].astype(F32)
+            prod = do_near[:, cols].astype(F32) * o_near[:, cols].astype(F32)
             high = prod.astype(BF16)
             low = (prod - high.astype(F32)).astype(BF16)
             row = (lax.dot_general(ones, high, NT, preferred_element_type=F32)
@@ -254,38 +266,30 @@
             rcopy(dsrc.at[t], dg_ref.at[t], col_send.at[0], d_recv.at[t],
                   place.in_column(t)).wait_recv()
     for cond, local in locals_:
-        pl.when(cond)(local.wait)
+        if cond is None:
+            local.wait()
+        else:
+            pl.when(cond)(local.wait)
     columns.finish()
     for here, away, copy, local in firsts:
         pl.when(away)(copy.wait_send)
 
 
-def grad_kernel(parents_ref, seg_ref, q_hbm, do_hbm, dg_ref, kv_hbm,
-                dkv_hbm, dq_ref,
-                acc, expd, kv, stage, q_all, do_all, qr, dor, tops, cuts, inv, dqt,
-                chain, in_sem, kv_sem, out_sem):
+def grad_kernel(parents_near, seg_ref, q_all, do_all, dg_ref, kv,
+                dkv_ref, dq_ref,
+                acc, expd, qr, dor, tops, cuts, inv, dqt, chain,
+                parents_ref, parents_sem):
     place = Place()
     x = place.x
     column = x * 4 + place.z
     first_block = (x - (NEAR - 1)) * (SECTION // BLOCK)
     factor = SCALE * LOG2E
 
-    loads = []
-    for slot in (2, 1, 0):
-        d = 2 - slot
-        rows = pl.ds(pl.multiple_of(((x + 4 - d) % 4) * SECTION, SECTION), SECTION)
-        for p in range(2):
-            copy = pltpu.make_async_copy(
-                kv_hbm.at[p, rows, :], kv.at[p, pl.ds(slot * SECTION, SECTION), :],
-                kv_sem.at[p, slot])
-            pl.when(x >= d)(copy.start)
-            loads.append((x >= d, copy))
-    q_copy = pltpu.make_async_copy(q_hbm, q_all, in_sem.at[0])
-    do_copy = pltpu.make_async_copy(do_hbm, do_all, in_sem.at[1])
-    q_copy.start()
-    do_copy.start()
-
+    parents_copy = pltpu.make_async_copy(parents_near, parents_ref, parents_sem)
+    parents_copy.start()
     n0 = jnp.sum((seg_ref[...] == 0).astype(jnp.int32))
+
+    parents_copy.wait()
 
     chains = [None] * 4
     free = jnp.int32(0)
@@ -321,21 +325,18 @@
                 acc[p, slot * SECTION:(slot + 1) * SECTION, :] = jnp.zeros((SECTION, D), F32)
     dqt[...] = jnp.zeros_like(dqt)
 
-    q_copy.wait()
-    do_copy.wait()
     for qb in range(4):
         for h in range(4):
             rows, cols = slice(qb * BLOCK, (qb + 1) * BLOCK), slice(h * D, (h + 1) * D)
             qr[qb * ROWS + h * D:qb * ROWS + (h + 1) * D, :] = q_all[rows, cols]
             dor[qb * ROWS + h * D:qb * ROWS + (h + 1) * D, :] = do_all[rows, cols]
-    for cond, copy in loads:
-        pl.when(cond)(copy.wait)
 
     def block_rows(b):
         return pl.ds(pl.multiple_of((b - first_block) * BLOCK, BLOCK), BLOCK)
 
     def gathered(p, blocks):
-        return jnp.concatenate([kv[p, block_rows(b), :] for b in blocks], axis=0)
+        return jnp.concatenate(
+            [kv[p, pl.ds(pl.multiple_of(b * BLOCK, BLOCK), BLOCK), :] for b in blocks], axis=0)
 
     def row_of(q):
         return pl.ds(pl.multiple_of(q * 8, 8), 1)
@@ -494,68 +495,65 @@
 
     lax.fori_loop(0, 2, one_half, 0)
 
-    stores = []
     for slot in range(NEAR):
-        for p, by in ((0, SCALE), (1, 1.0)):
-            at = slice(slot * SECTION, (slot + 1) * SECTION)
-            copy = pltpu.make_async_copy(
-                stage.at[p, pl.ds(slot * SECTION, SECTION), :], dkv_hbm.at[p, slot],
-                out_sem.at[p, slot])
-
-            @pl.when(x >= 2 - slot)
-            def _():
-                stage[p, at, :] = (acc[p, at, :] * by).astype(BF16)
-                copy.start()
-            stores.append((x >= 2 - slot, copy))
+        @pl.when(x >= 2 - slot)
+        def _():
+            for p, by in ((0, SCALE), (1, 1.0)):
+                at = slice(slot * SECTION, (slot + 1) * SECTION)
+                dkv_ref[p, slot] = (acc[p, at, :] * by).astype(BF16)
     for qb in range(4):
         for h in range(4):
             part = dqt[qb * D:(qb + 1) * D, h * D:(h + 1) * D].T * SCALE
             dq_ref[qb * BLOCK:(qb + 1) * BLOCK, h * D:(h + 1) * D] = part.astype(BF16)
-    for cond, copy in stores:
-        pl.when(cond)(copy.wait)
 
 
 def home_kernel(dkv_ref, dq_ref,
                 qg_ref, kg_ref, vg_ref,
-                own, sib, acc, snd, hop, rx, rz, rzz, rx2, done,
-                col_send, q_recv, local_sem, own_sem, sib_send, sib_recv,
+                sib, acc, snd, hop, rx, rz, rzz, rx2, done,
+                col_send, q_recv, local_sem, sib_send, sib_recv,
                 send_sems, rx_recv, rz_recv, rzz_recv, rx2_recv, end_send, end_recv):
     place = Place()
     x, z, core = place.x, place.z, place.core
     greet(place)
     sibling = place.at(core=1 - core)
 
-    def section(p, d):
-        return dkv_ref.at[p, 2 - d]
-
-    sib_copies = []
-    own_copies = []
-    for d in (2, 1, 0):
-        copy = rcopy(section(1 - core, d), sib.at[d], sib_send.at[d], sib_recv.at[d], sibling)
-        mine = pltpu.make_async_copy(section(core, d), own.at[d], own_sem.at[d])
-        pl.when(x >= d)(copy.start)
-        pl.when(x >= d)(mine.start)
-        sib_copies.append((d, copy))
-        own_copies.append((d, mine))
+    def rows_at(dz):
+        return pl.ds(pl.multiple_of(((z + dz) % 4) * COLUMN, COLUMN), COLUMN)
+
+    def share(p):
+        order = [(d, dz) for dz in FAR_FIRST for d in (2, 1, 0)]
+        if p == 1:
+            order = [(d, dz) for d in (2, 1, 0) for dz in FAR_FIRST]
+        copies = []
+        for d, dz in order:
+            copy = rcopy(dkv_ref.at[p, 2 - d, rows_at(dz), :], sib.at[d, rows_at(dz), :],
+                         sib_send.at[d, dz], sib_recv.at[d, dz], sibling)
+            pl.when(x >= d)(copy.start)
+            copies.append((d, copy))
+        return copies
+
+    pl.when(core == 1)(lambda: share(0) and None)
+    pl.when(core == 0)(lambda: share(1) and None)
 
     columns = Sends(col_send)
     col = pl.multiple_of(place.own * ROWS, ROWS)
     target = qg_ref.at[:, pl.ds(col, ROWS)]
-    for t in range(8):
-        src = dq_ref.at[pl.ds(place.home_row(t), 64), :]
-        columns.start(place.own != t, src, target, q_recv.at[place.own], place.in_column(t))
-        pl.when(place.own == t)(pltpu.make_async_copy(src, target, local_sem.at[0]).start)
-
-    for (d, copy), (_, mine) in zip(sib_copies, own_copies):
-        @pl.when(x >= d)
-        def _():
-            mine.wait()
-            copy.wait_recv()
-            both = own[d].astype(F32) + sib[d].astype(F32)
-            acc[d] = both
-            snd[d] = both.astype(BF16)
-
-    my_rows = pl.ds(pl.multiple_of(z * COLUMN, COLUMN), COLUMN)
+    for away in (4, 5, 2, 3, 6, 7, 1):
+        t = ((place.y + away // 2) % 4) * 2 + (core + away) % 2
+        src = dq_ref.at[pl.ds(pl.multiple_of(place.home_row(t), 64), 64), :]
+        columns.start(None, src, target, q_recv.at[place.own], place.in_column(t))
+    src = dq_ref.at[pl.ds(pl.multiple_of(place.home_row(), 64), 64), :]
+    stay = pltpu.make_async_copy(src, target, local_sem.at[0])
+    stay.start()
+
+    def both(p, d, dz):
+        part = sib.at[d, rows_at(dz), :]
+        rcopy(part, part, sib_send.at[d, dz], sib_recv.at[d, dz], sibling).wait_recv()
+        return dkv_ref[p, 2 - d, rows_at(dz), :].astype(F32) + part[...].astype(F32)
+
+    def arrived(ref, sem):
+        rcopy(ref, ref, send_sems.at[0], sem, sibling).wait_recv()
+        return ref[...].astype(F32)
 
     def finish(p, out_ref, total):
         done[...] = total.astype(BF16)
@@ -570,63 +568,67 @@
             pl.when(here)(local.wait)
             pl.when(jnp.logical_not(here))(copy.wait_send)
 
-    @pl.when(core == 0)
-    def _():
+    def keys_home():
         sends = Sends(send_sems)
-        for d in (2, 1):
-            sends.start(x >= d, snd.at[d], rx.at[d - 1], rx_recv.at[d - 1],
-                        place.at(x=(x + 4 - d) % 4))
+        for dz in FAR_FIRST:
+            for d in (2, 1):
+                @pl.when(x >= d)
+                def _():
+                    snd[d, rows_at(dz), :] = both(0, d, dz).astype(BF16)
+                sends.start(x >= d, snd.at[d, rows_at(dz), :], rx.at[d - 1, rows_at(dz), :],
+                            rx_recv.at[d - 1, dz], place.at(x=(x + 4 - d) % 4))
+            acc[0, rows_at(dz), :] = both(0, 0, dz)
+        for dz in FAR_FIRST:
+            for d in (1, 2):
+                @pl.when(x + d <= 3)
+                def _():
+                    acc[0, rows_at(dz), :] += arrived(rx.at[d - 1, rows_at(dz), :],
+                                                      rx_recv.at[d - 1, dz])
+            if dz:
+                hop[rows_at(dz), :] = acc[0, rows_at(dz), :].astype(BF16)
+                sends.start(None, hop.at[rows_at(dz), :], rz.at[dz - 1], rz_recv.at[dz - 1],
+                            place.at(z=(z + dz) % 4))
+        total = acc[0, rows_at(0), :]
+        for dz in (1, 3, 2):
+            total = total + arrived(rz.at[dz - 1], rz_recv.at[dz - 1])
+        finish(0, kg_ref, total)
+        sends.finish()
+
+    def values_home():
+        sends = Sends(send_sems)
+        for d in (2, 1, 0):
+            for dz in (2, 1, 3):
+                @pl.when(x >= d)
+                def _():
+                    snd[d, rows_at(dz), :] = both(1, d, dz).astype(BF16)
+                sends.start(x >= d, snd.at[d, rows_at(dz), :], rzz.at[dz - 1, d],
+                            rzz_recv.at[dz - 1, d], place.at(z=(z + dz) % 4))
+
+            @pl.when(x >= d)
+            def _():
+                acc[d, rows_at(0), :] = both(1, d, 0)
+        for d in (2, 1, 0):
+            @pl.when(x >= d)
+            def _():
+                part = acc[d, rows_at(0), :]
+                for dz in (1, 3, 2):
+                    part = part + arrived(rzz.at[dz - 1, d], rzz_recv.at[dz - 1, d])
+                if d == 0:
+                    acc[0, rows_at(0), :] = part
+                else:
+                    hop[d * COLUMN:(d + 1) * COLUMN, :] = part.astype(BF16)
+            if d > 0:
+                sends.start(x >= d, hop.at[pl.ds(d * COLUMN, COLUMN), :], rx2.at[d - 1],
+                            rx2_recv.at[d - 1], place.at(x=(x + 4 - d) % 4))
         for d in (1, 2):
             @pl.when(x + d <= 3)
             def _():
-                rcopy(snd.at[d], rx.at[d - 1], send_sems.at[0], rx_recv.at[d - 1],
-                      sibling).wait_recv()
-                acc[0] += rx[d - 1].astype(F32)
-        hop[...] = acc[0].astype(BF16)
-        for d in (1, 3, 2):
-            zz = (z + d) % 4
-            src = hop.at[pl.ds(pl.multiple_of(zz * COLUMN, COLUMN), COLUMN), :]
-            sends.start(None, src, rz.at[d - 1], rz_recv.at[d - 1], place.at(z=zz))
-        total = acc[0, my_rows, :]
-        for d in (1, 3, 2):
-            rcopy(rz.at[d - 1], rz.at[d - 1], send_sems.at[0], rz_recv.at[d - 1],
-                  sibling).wait_recv()
-            total = total + rz[d - 1].astype(F32)
-        finish(0, kg_ref, total)
+                acc[0, rows_at(0), :] += arrived(rx2.at[d - 1], rx2_recv.at[d - 1])
+        finish(1, vg_ref, acc[0, rows_at(0), :])
         sends.finish()
 
-    @pl.when(core == 1)
-    def _():
-        sends = Sends(send_sems)
-        for e in (2, 1, 0):
-            for d in (1, 3, 2):
-                zz = (z + d) % 4
-                src = snd.at[e, pl.ds(pl.multiple_of(zz * COLUMN, COLUMN), COLUMN), :]
-                sends.start(x >= e, src, rzz.at[d - 1, e], rzz_recv.at[d - 1, e], place.at(z=zz))
-        total = None
-        for e in (2, 1, 0):
-            @pl.when(x >= e)
-            def _():
-                part = acc[e, my_rows, :]
-                for d in (1, 3, 2):
-                    rcopy(rzz.at[d - 1, e], rzz.at[d - 1, e], send_sems.at[0],
-                          rzz_recv.at[d - 1, e], sibling).wait_recv()
-                    part = part + rzz[d - 1, e].astype(F32)
-                if e == 0:
-                    acc[0, my_rows, :] = part
-                else:
-                    hop[e * COLUMN:(e + 1) * COLUMN, :] = part.astype(BF16)
-            if e > 0:
-                sends.start(x >= e, hop.at[pl.ds(e * COLUMN, COLUMN), :], rx2.at[e - 1],
-                            rx2_recv.at[e - 1], place.at(x=(x + 4 - e) % 4))
-        for d in (1, 2):
-            @pl.when(x + d <= 3)
-            def _():
-                rcopy(rx2.at[d - 1], rx2.at[d - 1], send_sems.at[0], rx2_recv.at[d - 1],
-                      sibling).wait_recv()
-                acc[0, my_rows, :] += rx2[d - 1].astype(F32)
-        finish(1, vg_ref, acc[0, my_rows, :])
-        sends.finish()
+    pl.when(core == 0)(keys_home)
+    pl.when(core == 1)(values_home)
 
     for p, out_ref in ((0, kg_ref), (1, vg_ref)):
         here = (place.ylo == core) & (core == p)
@@ -638,14 +640,18 @@
             src = dq_ref.at[pl.ds(0, 64), :]
             rcopy(src, qg_ref.at[:, pl.ds(t * ROWS, ROWS)], col_send.at[0], q_recv.at[t],
                   sibling).wait_recv()
-    pltpu.make_async_copy(dq_ref.at[pl.ds(0, 64), :], target, local_sem.at[0]).wait()
+    stay.wait()
     columns.finish()
-    for d, copy in sib_copies:
-        pl.when(x >= d)(copy.wait_send)
+    for d in range(NEAR):
+        for dz in range(4):
+            part = dkv_ref.at[0, 2 - d, rows_at(dz), :]
+            pl.when(x >= d)(rcopy(part, part, sib_send.at[d, dz], sib_recv.at[d, dz],
+                                  sibling).wait_send)
 
 
 ANY = pl.BlockSpec(memory_space=pl.ANY)
 VMEM = pl.BlockSpec(memory_space=pltpu.VMEM)
+HBM = pl.BlockSpec(memory_space=pltpu.HBM)
 SMEM = pl.BlockSpec(memory_space=pltpu.SMEM)
 DMA = pltpu.SemaphoreType.DMA
 MIB = 1 << 20
@@ -655,47 +661,44 @@
     return jax.ShapeDtypeStruct(shape, dtype)
 
 
-def spread(q, do, o, k, v):
+def spread(q, do, o, k, v, seg, parents):
     return pl.pallas_call(
         spread_kernel,
-        out_shape=(struct((COLUMN, ROWS), BF16), struct((COLUMN, ROWS), BF16),
-                   struct((8, 8, 128), F32), struct((2, TOKENS, D), BF16)),
-        in_specs=[ANY, VMEM, VMEM, ANY, ANY],
-        out_specs=(ANY, ANY, ANY, ANY),
+        out_shape=(pltpu.VMEM((COLUMN, ROWS), BF16), pltpu.VMEM((COLUMN, ROWS), BF16),
+                   pltpu.VMEM((8, 8, 128), F32), pltpu.VMEM((2, TOKENS, D), BF16),
+                   pltpu.VMEM((64, 128), jnp.int32), pltpu.VMEM((64,), jnp.int32)),
+        in_specs=[HBM] * 7,
+        out_specs=(VMEM,) * 6,
         scratch_shapes=[
+            pltpu.VMEM((64, 4096), BF16), pltpu.VMEM((64, 4096), BF16), DMA((4,)),
             pltpu.VMEM((8, 8, 128), F32),
             DMA((24,)), DMA((8,)), DMA((8,)), DMA((8,)), DMA((4,)),
             DMA((2,)), DMA((2,)), DMA((32,)), DMA((16,)), DMA((16,)),
         ],
         compiler_params=pltpu.CompilerParams(
-            collective_id=0, has_side_effects=True, vmem_limit_bytes=60 * MIB),
+            collective_id=0, has_side_effects=True, vmem_limit_bytes=56 * MIB),
         name="spread",
-    )(q, do, o, k, v)
+    )(q, do, o, k, v, seg, parents)
 
 
 def grads(parents, seg, q, do, dg, kv):
     return pl.pallas_call(
         grad_kernel,
-        out_shape=(struct((2, NEAR, SECTION, D), BF16), struct((COLUMN, ROWS), BF16)),
-        in_specs=[SMEM, VMEM, ANY, ANY, VMEM, ANY],
-        out_specs=(ANY, VMEM),
+        out_shape=(pltpu.VMEM((2, NEAR, SECTION, D), BF16), pltpu.VMEM((COLUMN, ROWS), BF16)),
+        in_specs=[VMEM] * 6,
+        out_specs=(VMEM, VMEM),
         scratch_shapes=[
             pltpu.VMEM((2, NEAR * SECTION, D), F32),
             pltpu.VMEM((SLOTS * GROUP * BLOCK, ROWS), F32),
-            pltpu.VMEM((2, NEAR * SECTION, D), BF16),
-            pltpu.VMEM((2, NEAR * SECTION, D), BF16),
-            pltpu.VMEM((COLUMN, ROWS), BF16),
-            pltpu.VMEM((COLUMN, ROWS), BF16),
             pltpu.VMEM((4 * ROWS, D), BF16),
             pltpu.VMEM((4 * ROWS, D), BF16),
             pltpu.VMEM((SLOTS * 8, ROWS), F32),
             pltpu.VMEM((16, ROWS), F32),
             pltpu.VMEM((16, ROWS), F32),
             pltpu.VMEM((4 * D, ROWS), F32),
-            pltpu.SMEM((256,), jnp.int32),
-            DMA((2,)), DMA((2, NEAR)), DMA((2, NEAR)),
+            pltpu.SMEM((256,), jnp.int32), pltpu.SMEM((64,), jnp.int32), DMA,
         ],
-        compiler_params=pltpu.CompilerParams(vmem_limit_bytes=60 * MIB),
+        compiler_params=pltpu.CompilerParams(vmem_limit_bytes=38 * MIB),
         name="grads",
     )(parents, seg, q, do, dg, kv)
 
@@ -703,11 +706,11 @@
 def home(dkv, dq):
     return pl.pallas_call(
         home_kernel,
-        out_shape=(struct((64, 4096), BF16), struct((256, D), BF16), struct((256, D), BF16)),
-        in_specs=[ANY, ANY],
-        out_specs=(ANY, ANY, ANY),
+        out_shape=(pltpu.VMEM((64, 4096), BF16), pltpu.VMEM((256, D), BF16),
+                   pltpu.VMEM((256, D), BF16)),
+        in_specs=[VMEM, VMEM],
+        out_specs=(VMEM,) * 3,
         scratch_shapes=[
-            pltpu.VMEM((NEAR, SECTION, D), BF16),
             pltpu.VMEM((NEAR, SECTION, D), BF16),
             pltpu.VMEM((NEAR, SECTION, D), F32),
             pltpu.VMEM((NEAR, SECTION, D), BF16),
@@ -717,23 +720,18 @@
             pltpu.VMEM((3, NEAR, COLUMN, D), BF16),
             pltpu.VMEM((2, COLUMN, D), BF16),
             pltpu.VMEM((COLUMN, D), BF16),
-            DMA((8,)), DMA((8,)), DMA((2,)), DMA((3,)), DMA((3,)), DMA((3,)),
-            DMA((12,)), DMA((2,)), DMA((3,)), DMA((3, 3)), DMA((2,)), DMA((2,)), DMA((2,)),
+            DMA((8,)), DMA((8,)), DMA((2,)), DMA((3, 4)), DMA((3, 4)),
+            DMA((16,)), DMA((2, 4)), DMA((3,)), DMA((3, 3)), DMA((2,)), DMA((2,)),
+            DMA((2,)),
         ],
         compiler_params=pltpu.CompilerParams(
-            collective_id=1, has_side_effects=True, vmem_limit_bytes=60 * MIB),
+            collective_id=1, has_side_effects=True, vmem_limit_bytes=24 * MIB),
         name="home",
     )(dkv, dq)
 
 
 def hand_over_kernel(*refs):
-    copies = []
-    for n in range(3):
-        src, dst = refs[n], refs[3 + n]
-        rows = src.shape[0] // 4
-        for i in range(4):
-            at = pl.ds(i * rows, rows)
-            copies.append(pltpu.make_async_copy(src.at[at, :], dst.at[at, :], refs[6].at[n, i]))
+    copies = [pltpu.make_async_copy(refs[n], refs[3 + n], refs[6].at[n]) for n in range(3)]
     for copy in copies:
         copy.start()
     for copy in copies:
@@ -744,17 +742,18 @@
     return pl.pallas_call(
         hand_over_kernel,
         out_shape=tuple(struct(a.shape, a.dtype) for a in arrays),
-        in_specs=[ANY] * 3,
-        out_specs=(ANY,) * 3,
-        scratch_shapes=[DMA((3, 4))],
-        compiler_params=pltpu.CompilerParams(vmem_limit_bytes=60 * MIB),
+        in_specs=[VMEM] * 3,
+        out_specs=(HBM,) * 3,
+        scratch_shapes=[DMA((3,))],
+        compiler_params=pltpu.CompilerParams(vmem_limit_bytes=8 * MIB),
         name="hand_over",
     )(*arrays)
 
 
 def local(query_rows, key_rows, value_rows, attn_output, out_grad, segments, parents):
-    q, do, dg, kv = spread(query_rows, out_grad, attn_output, key_rows, value_rows)
-    dkv, dq = grads(parents, segments.reshape(64, 128), q, do, dg, kv)
+    q, do, dg, kv, seg, parents = spread(
+        query_rows, out_grad, attn_output, key_rows, value_rows, segments.reshape(64, 128), parents)
+    dkv, dq = grads(parents, seg, q, do, dg, kv)
     return hand_over(*home(dkv, dq))
 
 

time: 115 us -> 82.5 us (0.72)
  Pallas kernels: 113 us -> 81.7 us
    pallas_call x1, Pallas kernels: 21.1 us -> 0.85 us  [hand_over(): pl.pallas_call(hand_over_kernel, out_shape=tuple((struct(a.shape, a.dtype...]
    pallas_call x3, Pallas kernels: 92.1 us -> 80.8 us  [the longest x1 38.7 us: home(): pl.pallas_call(home_kernel, out_shape=(pltpu.VMEM((64, 4096), BF16), pltp...]
where the time goes in v4:
time: 82.5 us; the launch traced here: 82.4 us
  Pallas kernels  81.7 us (99%)
    pallas_call x1, Pallas kernels, home(): pl.pallas_call(home_kernel, out_shape=(pltpu.VMEM((64, 4096), BF16), pltp...  38.7 us
    pallas_call x1, Pallas kernels, spread(): pl.pallas_call(spread_kernel, out_shape=(pltpu.VMEM((COLUMN, ROWS), BF16)...  23 us
    pallas_call x1, Pallas kernels, grads(): pl.pallas_call(grad_kernel, out_shape=(pltpu.VMEM((2, NEAR, SECTION, D),...  19.2 us

profile of v4, /device:TPU:10, one launch (start us, length us, event | category | flops | bytes accessed | tf_op | source)
XLA Modules:
  0.0 82.4 jit_solution(11120271365169263453)
XLA Ops:
  0.6 23.0 %spread.1 = (bf16[512,512]{1,0:T(8,128)(2,1)S(1)}, bf16[512,512]{1,0:T(8,128)(2,1)S(1)}, f32[8,8,128]{2,1,0:T(8,128)S(1)}, bf16[2,8192,128]{2,1,0:T(8,128)(2,1)S...) custom-call(bf16[64,4096]{1,0:T(8,128)(2,1)} %q_ref.1, bf16[64,4096]{1,0:T(8,128)(2,1)} %do_ref.1, bf16[64,4096]{1,0:T(8,128)(2,1)} %o_ref.1, ...), custom_call_target="tpu_custom_call" | custom-call | tf_op jit(solution)/shard_map/spread/pallas_call | solution.py:665
  23.6 19.2 %grads.1 = (bf16[2,3,2048,128]{3,2,1,0:T(8,128)(2,1)S(1)}, bf16[512,512]{1,0:T(8,128)(2,1)S(1)}) custom-call(s32[64]{0:T(128)S(1)} %get-tuple-element.14.parents_near, s32[64,128]{1,0:T(8,128)S(1)} %get-tuple-element.15.seg_ref, bf16[512,512]{1,0:T(8,128)(2,1)S(1)} %get-tuple-element.16.q_all, bf16[512,512]{1,0:T(8,128)(2,1)S(1)} %get-tuple-element.17.do_all, ...), custom_call_target="tpu_custom_call" | custom-call | tf_op jit(solution)/shard_map/grads/pallas_call | solution.py:685
  42.8 38.7 %home.1 = (bf16[64,4096]{1,0:T(8,128)(2,1)S(1)}, bf16[256,128]{1,0:T(8,128)(2,1)S(1)}, bf16[256,128]{1,0:T(8,128)(2,1)S(1)}) custom-call(bf16[2,3,2048,128]{3,2,1,0:T(8,128)(2,1)S(1)} %get-tuple-element.20.dkv_ref, bf16[512,512]{1,0:T(8,128)(2,1)S(1)} %get-tuple-element.21.dq_ref), custom_call_target="tpu_custom_call" | custom-call | tf_op jit(solution)/shard_map/home/pallas_call | solution.py:707
  81.5 0.9 %hand_over.1 = (bf16[64,4096]{1,0:T(8,128)(2,1)}, bf16[256,128]{1,0:T(8,128)(2,1)}, bf16[256,128]{1,0:T(8,128)(2,1)}) custom-call(bf16[64,4096]{1,0:T(8,128)(2,1)S(1)} %get-tuple-element.22.refs_0_, bf16[256,128]{1,0:T(8,128)(2,1)S(1)} %get-tuple-element.23.refs_1_, bf16[256,128]{1,0:T(8,128)(2,1)S(1)} %get-tuple-element.24.refs_2_), custom_call_target="tpu_custom_call" | custom-call | tf_op jit(solution)/shard_map/hand_over/pallas_call | solution.py:742

commit v5 on v4

--- a/solution.py
+++ b/solution.py
@@ -15,6 +15,7 @@
 SECTION = 2048
 NEAR = 3
 FAR_FIRST = (2, 1, 3, 0)
+RELAYED = (0, 1)
 GROUP = 4
 SCORES_AT_ONCE = 4
 GRADS_AT_ONCE = 2
@@ -62,7 +63,7 @@
         return (((t // 2) % 2) * 2 + t // 4) * 128 + (t % 2) * 64
 
 
-def greet(place):
+def greet(place, homeward=False):
     barrier = pltpu.get_barrier_semaphore()
     for t in range(8):
         @pl.when(place.own != t)
@@ -73,7 +74,21 @@
             barrier, inc=1, device_id=place.at(x=(place.x + step) % 4), device_id_type=MESH)
         pl.semaphore_signal(
             barrier, inc=1, device_id=place.at(z=(place.z + step) % 4), device_id_type=MESH)
-    pl.semaphore_wait(barrier, 13)
+    if not homeward:
+        pl.semaphore_wait(barrier, 13)
+        return
+    for step in range(1, 4):
+        pl.semaphore_signal(
+            barrier, inc=1, device_id=place.at(z=(place.z + step) % 4, ylo=place.core, core=0),
+            device_id_type=MESH)
+    for d in (1, 2):
+        @pl.when(place.x + d <= 3)
+        def _():
+            pl.semaphore_signal(
+                barrier, inc=1,
+                device_id=place.at(x=(place.x + d) % 4, ylo=place.core, core=1),
+                device_id_type=MESH)
+    pl.semaphore_wait(barrier, 13 + jnp.where(place.core == 0, 6, 2 * jnp.minimum(place.x, 2)))
 
 
 def rcopy(src, dst, send, recv, device):
@@ -106,7 +121,7 @@
 def spread_kernel(q_ref, do_ref, o_ref, k_ref, v_ref, seg_ref, parents_ref,
                   qg_ref, dog_ref, dg_ref, kv_ref, seg_near, parents_near,
                   do_near, o_near, near_sem, dsrc, col_send, q_recv, do_recv, d_recv, local_sem,
-                  first_send, first_recv, piece_send, prim_recv, sib_recv):
+                  first_send, first_recv, piece_send, prim_recv, sib_recv, dot_send):
     place = Place()
     x, z, core = place.x, place.z, place.core
     nears = [pltpu.make_async_copy(do_ref, do_near, near_sem.at[0]),
@@ -133,19 +148,21 @@
     my_row = pl.multiple_of(place.home_row(), 64)
     columns = Sends(col_send)
     locals_ = []
-    for away in (4, 5, 2, 3, 6, 7, 1, 0):
-        t = ((place.y + away // 2) % 4) * 2 + (core + away) % 2
-        cols = pl.ds(pl.multiple_of(t * ROWS, ROWS), ROWS)
-        for n, (src, dst, recv) in enumerate(
-                ((q_ref, qg_ref, q_recv), (do_ref, dog_ref, do_recv))):
-            target = dst.at[pl.ds(my_row, 64), :]
+
+    def across(src, dst, recv, sem):
+        target = dst.at[pl.ds(my_row, 64), :]
+        for away in (4, 5, 2, 3, 6, 7, 1, 0):
+            t = ((place.y + away // 2) % 4) * 2 + (core + away) % 2
+            cols = pl.ds(pl.multiple_of(t * ROWS, ROWS), ROWS)
             if away:
                 columns.start(None, src.at[:, cols], target, recv.at[place.own],
                               place.in_column(t))
             else:
-                local = pltpu.make_async_copy(src.at[:, cols], target, local_sem.at[n])
+                local = pltpu.make_async_copy(src.at[:, cols], target, sem)
                 local.start()
-                locals_.append((None, local))
+                locals_.append(local)
+
+    across(q_ref, qg_ref, q_recv, local_sem.at[0])
 
     lane = lax.broadcasted_iota(jnp.int32, (8, 128), 1)
     line = lax.broadcasted_iota(jnp.int32, (8, 128), 0)
@@ -165,13 +182,15 @@
             row = jnp.concatenate([row, row], axis=1)
             tile = jnp.where(mine & (line == r), row, tile)
         dsrc[t] = tile
+    dots = Sends(dot_send)
+    target = dg_ref.at[place.own]
     for t in range(8):
-        target = dg_ref.at[place.own]
-        columns.start(place.own != t, dsrc.at[t], target, d_recv.at[place.own],
-                      place.in_column(t))
-        local = pltpu.make_async_copy(dsrc.at[t], target, local_sem.at[2])
-        pl.when(place.own == t)(local.start)
-        locals_.append((place.own == t, local))
+        dots.start(place.own != t, dsrc.at[t], target, d_recv.at[place.own],
+                   place.in_column(t))
+    stay = pltpu.make_async_copy(dsrc.at[place.own], target, local_sem.at[2])
+    stay.start()
+
+    across(do_ref, dog_ref, do_recv, local_sem.at[1])
 
     for half in range(2):
         here = (place.ylo == core) & (place.ylo == half)
@@ -181,8 +200,11 @@
     for here, away, copy, local in firsts:
         pl.when(here)(local.wait)
 
-    def piece(p, xx, zz):
-        return kv_ref.at[p, pl.ds(pl.multiple_of((xx * 4 + zz) * COLUMN, COLUMN), COLUMN), :]
+    def piece(p, xx, zz, half=None):
+        start = pl.multiple_of((xx * 4 + zz) * COLUMN, COLUMN)
+        if half is None:
+            return kv_ref.at[p, pl.ds(start, COLUMN), :]
+        return kv_ref.at[p, pl.ds(pl.multiple_of(start + half * 256, 256), 256), :]
 
     sibling = place.at(core=1 - core)
 
@@ -193,37 +215,47 @@
             part = piece(c, xx, zz)
             sends.start(cond, part, part, sib_recv.at[xx * 4 + zz], sibling)
 
-        def along_x(cond, xx, zz):
+        def along_x(zz, dz):
+            part = piece(c, x, zz)
+            recv = prim_recv.at[x * 4 + zz, 0]
+            sends.start(x <= 2, part, part, recv, place.at(x=(x + 1) % 4))
+            step = 3 if c == 0 and dz in RELAYED else 2
+            sends.start(x <= 1, part, part, recv, place.at(x=(x + step) % 4))
+
+        def pass_on(dz):
+            xx, zz = (x + 1) % 4, (z + dz) % 4
+            between = (x == 0) | (x == 3)
+            arrive(between, xx, zz)
             part = piece(c, xx, zz)
-            for d in (1, 2):
-                ok = x + d <= 3
-                ok = ok if cond is None else ok & cond
-                sends.start(ok, part, part, prim_recv.at[xx * 4 + zz],
-                            place.at(x=(x + d) % 4))
-
-        def along_z(cond, xx, zz):
-            part = piece(c, xx, zz)
+            sends.start(between, part, part, prim_recv.at[xx * 4 + zz, 0],
+                        place.at(x=(x + 3) % 4))
+
+        def along_z(cond, xx):
+            part = piece(c, xx, z)
             for d in (1, 3, 2):
-                sends.start(cond, part, part, prim_recv.at[xx * 4 + zz],
+                sends.start(cond, part, part, prim_recv.at[xx * 4 + z, 0],
                             place.at(z=(z + d) % 4))
 
-        def arrive(cond, xx, zz):
-            part = piece(c, xx, zz)
-            wait = rcopy(part, part, piece_send.at[0], prim_recv.at[xx * 4 + zz], sibling)
-            if cond is None:
-                wait.wait_recv()
-            else:
-                pl.when(cond)(wait.wait_recv)
+        def arrive(cond, xx, zz, halves=False):
+            parts = [piece(c, xx, zz, h) for h in (0, 1)] if halves else [piece(c, xx, zz)]
+            for h, part in enumerate(parts):
+                wait = rcopy(part, part, piece_send.at[0], prim_recv.at[xx * 4 + zz, h], sibling)
+                if cond is None:
+                    wait.wait_recv()
+                else:
+                    pl.when(cond)(wait.wait_recv)
 
         if c == 0:
-            along_z(None, x, z)
-            along_x(None, x, z)
+            along_z(None, x)
+            along_x(z, 0)
             share(None, x, z)
             for dz in (1, 3, 2):
                 zz = (z + dz) % 4
                 arrive(None, x, zz)
-                along_x(None, x, zz)
+                along_x(zz, dz)
                 share(None, x, zz)
+                if {1: 0, 3: 1, 2: 3}[dz] in RELAYED:
+                    pass_on({1: 0, 3: 1, 2: 3}[dz])
             for dz in (0, 1, 3, 2):
                 zz = (z + dz) % 4
                 for d in (1, 2):
@@ -231,20 +263,20 @@
                     arrive(x >= d, xx, zz)
                     share(x >= d, xx, zz)
         else:
-            along_x(None, x, z)
-            along_z(None, x, z)
+            along_x(z, 0)
+            along_z(None, x)
             share(None, x, z)
             for d in (1, 2):
                 xx = (x + 4 - d) % 4
                 arrive(x >= d, xx, z)
-                along_z(x >= d, xx, z)
+                along_z(x >= d, xx)
                 share(x >= d, xx, z)
-            for d in range(NEAR):
-                xx = (x + 4 - d) % 4
-                for dz in (1, 3, 2):
-                    zz = (z + dz) % 4
-                    arrive(None if d == 0 else x >= d, xx, zz)
-                    share(None if d == 0 else x >= d, xx, zz)
+            for dz in (1, 3, 2):
+                zz = (z + dz) % 4
+                for d in range(NEAR):
+                    xx = (x + 4 - d) % 4
+                    arrive(x >= d, xx, zz)
+                    share(x >= d, xx, zz)
         for d in range(NEAR):
             xx = (x + 4 - d) % 4
             for zz in range(4):
@@ -263,13 +295,13 @@
             for src, dst, recv in ((q_ref, qg_ref, q_recv), (do_ref, dog_ref, do_recv)):
                 rcopy(src.at[:, pl.ds(0, ROWS)], dst.at[pl.ds(row, 64), :], col_send.at[0],
                       recv.at[t], place.in_column(t)).wait_recv()
-            rcopy(dsrc.at[t], dg_ref.at[t], col_send.at[0], d_recv.at[t],
-                  place.in_column(t)).wait_recv()
-    for cond, local in locals_:
-        if cond is None:
-            local.wait()
-        else:
-            pl.when(cond)(local.wait)
+    for local in locals_:
+        local.wait()
+    for t in range(8):
+        pl.when(place.own != t)(rcopy(dsrc.at[t], dg_ref.at[t], dot_send.at[0], d_recv.at[t],
+                                      place.in_column(t)).wait_recv)
+    stay.wait()
+    dots.finish()
     columns.finish()
     for here, away, copy, local in firsts:
         pl.when(away)(copy.wait_send)
@@ -509,12 +541,12 @@
 
 def home_kernel(dkv_ref, dq_ref,
                 qg_ref, kg_ref, vg_ref,
-                sib, acc, snd, hop, rx, rz, rzz, rx2, done,
+                sib, acc, snd, hop, rx, rz, rzz, rx2,
                 col_send, q_recv, local_sem, sib_send, sib_recv,
-                send_sems, rx_recv, rz_recv, rzz_recv, rx2_recv, end_send, end_recv):
+                send_sems, rx_recv, rz_recv, rzz_recv, rx2_recv):
     place = Place()
     x, z, core = place.x, place.z, place.core
-    greet(place)
+    greet(place, True)
     sibling = place.at(core=1 - core)
 
     def rows_at(dz):
@@ -555,18 +587,18 @@
         rcopy(ref, ref, send_sems.at[0], sem, sibling).wait_recv()
         return ref[...].astype(F32)
 
-    def finish(p, out_ref, total):
-        done[...] = total.astype(BF16)
+    def send_halves(sends, cond, src, start, landing, recv, x_to, z_to, stays):
         for half in range(2):
-            src = done.at[pl.ds(half * 256, 256), :]
-            here = (place.ylo == half) & (core == place.ylo)
-            copy = rcopy(src, out_ref, end_send.at[half], end_recv.at[p],
-                         place.at(ylo=half, core=place.ylo))
-            local = pltpu.make_async_copy(src, out_ref, local_sem.at[1])
-            pl.when(here)(local.start)
-            pl.when(jnp.logical_not(here))(copy.start)
-            pl.when(here)(local.wait)
-            pl.when(jnp.logical_not(here))(copy.wait_send)
+            rows = src.at[pl.ds(pl.multiple_of(start + half * 256, 256), 256), :]
+            away = cond
+            if stays:
+                here = (place.ylo == half) & (core == place.ylo)
+                local = pltpu.make_async_copy(rows, landing, local_sem.at[1])
+                pl.when(here)(local.start)
+                pl.when(here)(local.wait)
+                away = jnp.logical_not(here)
+            sends.start(away, rows, landing, recv,
+                        place.at(x=x_to, z=z_to, ylo=half, core=place.ylo))
 
     def keys_home():
         sends = Sends(send_sems)
@@ -584,14 +616,9 @@
                 def _():
                     acc[0, rows_at(dz), :] += arrived(rx.at[d - 1, rows_at(dz), :],
                                                       rx_recv.at[d - 1, dz])
-            if dz:
-                hop[rows_at(dz), :] = acc[0, rows_at(dz), :].astype(BF16)
-                sends.start(None, hop.at[rows_at(dz), :], rz.at[dz - 1], rz_recv.at[dz - 1],
-                            place.at(z=(z + dz) % 4))
-        total = acc[0, rows_at(0), :]
-        for dz in (1, 3, 2):
-            total = total + arrived(rz.at[dz - 1], rz_recv.at[dz - 1])
-        finish(0, kg_ref, total)
+            hop[rows_at(dz), :] = acc[0, rows_at(dz), :].astype(BF16)
+            send_halves(sends, None, hop, ((z + dz) % 4) * COLUMN, rz.at[dz], rz_recv.at[dz],
+                        x, (z + dz) % 4, dz == 0)
         sends.finish()
 
     def values_home():
@@ -613,27 +640,34 @@
                 part = acc[d, rows_at(0), :]
                 for dz in (1, 3, 2):
                     part = part + arrived(rzz.at[dz - 1, d], rzz_recv.at[dz - 1, d])
-                if d == 0:
-                    acc[0, rows_at(0), :] = part
-                else:
-                    hop[d * COLUMN:(d + 1) * COLUMN, :] = part.astype(BF16)
-            if d > 0:
-                sends.start(x >= d, hop.at[pl.ds(d * COLUMN, COLUMN), :], rx2.at[d - 1],
-                            rx2_recv.at[d - 1], place.at(x=(x + 4 - d) % 4))
-        for d in (1, 2):
-            @pl.when(x + d <= 3)
-            def _():
-                acc[0, rows_at(0), :] += arrived(rx2.at[d - 1], rx2_recv.at[d - 1])
-        finish(1, vg_ref, acc[0, rows_at(0), :])
+                hop[d * COLUMN:(d + 1) * COLUMN, :] = part.astype(BF16)
+            send_halves(sends, x >= d, hop, d * COLUMN, rx2.at[d], rx2_recv.at[d],
+                        (x + 4 - d) % 4, z, d == 0)
         sends.finish()
 
     pl.when(core == 0)(keys_home)
     pl.when(core == 1)(values_home)
 
-    for p, out_ref in ((0, kg_ref), (1, vg_ref)):
-        here = (place.ylo == core) & (core == p)
-        wait = rcopy(done.at[pl.ds(0, 256), :], out_ref, end_send.at[0], end_recv.at[p], sibling)
-        pl.when(jnp.logical_not(here))(wait.wait_recv)
+    def landed(ref, sem, p, stays):
+        wait = rcopy(ref, ref, send_sems.at[0], sem, sibling)
+        if stays:
+            here = (core == p) & (place.ylo == p)
+            pl.when(jnp.logical_not(here))(wait.wait_recv)
+        else:
+            wait.wait_recv()
+        return ref[...].astype(F32)
+
+    total = None
+    for dz in FAR_FIRST:
+        part = landed(rz.at[dz], rz_recv.at[dz], 0, dz == 0)
+        total = part if total is None else total + part
+    kg_ref[...] = total.astype(BF16)
+    acc[0, 0:256, :] = landed(rx2.at[0], rx2_recv.at[0], 1, True)
+    for d in (1, 2):
+        @pl.when(x + d <= 3)
+        def _():
+            acc[0, 0:256, :] += landed(rx2.at[d], rx2_recv.at[d], 1, False)
+    vg_ref[...] = acc[0, 0:256, :].astype(BF16)
     for t in range(8):
         @pl.when(place.own != t)
         def _():
@@ -673,7 +707,7 @@
             pltpu.VMEM((64, 4096), BF16), pltpu.VMEM((64, 4096), BF16), DMA((4,)),
             pltpu.VMEM((8, 8, 128), F32),
             DMA((24,)), DMA((8,)), DMA((8,)), DMA((8,)), DMA((4,)),
-            DMA((2,)), DMA((2,)), DMA((32,)), DMA((16,)), DMA((16,)),
+            DMA((2,)), DMA((2,)), DMA((32,)), DMA((16, 2)), DMA((16,)), DMA((8,)),
         ],
         compiler_params=pltpu.CompilerParams(
             collective_id=0, has_side_effects=True, vmem_limit_bytes=56 * MIB),
@@ -716,13 +750,11 @@
             pltpu.VMEM((NEAR, SECTION, D), BF16),
             pltpu.VMEM((SECTION, D), BF16),
             pltpu.VMEM((2, SECTION, D), BF16),
-            pltpu.VMEM((3, COLUMN, D), BF16),
+            pltpu.VMEM((4, 256, D), BF16),
             pltpu.VMEM((3, NEAR, COLUMN, D), BF16),
-            pltpu.VMEM((2, COLUMN, D), BF16),
-            pltpu.VMEM((COLUMN, D), BF16),
+            pltpu.VMEM((NEAR, 256, D), BF16),
             DMA((8,)), DMA((8,)), DMA((2,)), DMA((3, 4)), DMA((3, 4)),
-            DMA((16,)), DMA((2, 4)), DMA((3,)), DMA((3, 3)), DMA((2,)), DMA((2,)),
-            DMA((2,)),
+            DMA((20,)), DMA((2, 4)), DMA((4,)), DMA((3, 3)), DMA((3,)),
         ],
         compiler_params=pltpu.CompilerParams(
             collective_id=1, has_side_effects=True, vmem_limit_bytes=24 * MIB),

time: 82.5 us -> 70.8 us (0.86); the launches traced: 82.4 us -> 69.5 us
  Pallas kernels: 81.7 us -> 68.9 us
    pallas_call x1, Pallas kernels: 38.7 us -> 29.6 us  [home(): pl.pallas_call(home_kernel, out_shape=(pltpu.VMEM((64, 4096), BF16), pltp...]
    pallas_call x1, Pallas kernels: 19.2 us -> 16.1 us  [grads(): pl.pallas_call(grad_kernel, out_shape=(pltpu.VMEM((2, NEAR, SECTION, D),...]
where the time goes in v5:
time: 70.8 us; the launch traced here: 69.5 us
  Pallas kernels  68.9 us (97%)
    pallas_call x1, Pallas kernels, home(): pl.pallas_call(home_kernel, out_shape=(pltpu.VMEM((64, 4096), BF16), pltp...  29.6 us
    pallas_call x1, Pallas kernels, spread(): pl.pallas_call(spread_kernel, out_shape=(pltpu.VMEM((COLUMN, ROWS), BF16)...  22.4 us
    pallas_call x1, Pallas kernels, grads(): pl.pallas_call(grad_kernel, out_shape=(pltpu.VMEM((2, NEAR, SECTION, D),...  16.1 us

profile of v5, /device:TPU:10, one launch (start us, length us, event | category | flops | bytes accessed | tf_op | source)
XLA Modules:
  0.0 69.5 jit_solution(17165871071814975437)
XLA Ops:
  0.6 22.4 %spread.1 = (bf16[512,512]{1,0:T(8,128)(2,1)S(1)}, bf16[512,512]{1,0:T(8,128)(2,1)S(1)}, f32[8,8,128]{2,1,0:T(8,128)S(1)}, bf16[2,8192,128]{2,1,0:T(8,128)(2,1)S...) custom-call(bf16[64,4096]{1,0:T(8,128)(2,1)} %q_ref.1, bf16[64,4096]{1,0:T(8,128)(2,1)} %do_ref.1, bf16[64,4096]{1,0:T(8,128)(2,1)} %o_ref.1, ...), custom_call_target="tpu_custom_call" | custom-call | tf_op jit(solution)/shard_map/spread/pallas_call | solution.py:699
  23.0 16.1 %grads.1 = (bf16[2,3,2048,128]{3,2,1,0:T(8,128)(2,1)S(1)}, bf16[512,512]{1,0:T(8,128)(2,1)S(1)}) custom-call(s32[64]{0:T(128)S(1)} %get-tuple-element.14.parents_near, s32[64,128]{1,0:T(8,128)S(1)} %get-tuple-element.15.seg_ref, bf16[512,512]{1,0:T(8,128)(2,1)S(1)} %get-tuple-element.16.q_all, bf16[512,512]{1,0:T(8,128)(2,1)S(1)} %get-tuple-element.17.do_all, ...), custom_call_target="tpu_custom_call" | custom-call | tf_op jit(solution)/shard_map/grads/pallas_call | solution.py:719
  39.1 29.6 %home.1 = (bf16[64,4096]{1,0:T(8,128)(2,1)S(1)}, bf16[256,128]{1,0:T(8,128)(2,1)S(1)}, bf16[256,128]{1,0:T(8,128)(2,1)S(1)}) custom-call(bf16[2,3,2048,128]{3,2,1,0:T(8,128)(2,1)S(1)} %get-tuple-element.20.dkv_ref, bf16[512,512]{1,0:T(8,128)(2,1)S(1)} %get-tuple-element.21.dq_ref), custom_call_target="tpu_custom_call" | custom-call | tf_op jit(solution)/shard_map/home/pallas_call | solution.py:741
  68.7 0.9 %hand_over.1 = (bf16[64,4096]{1,0:T(8,128)(2,1)}, bf16[256,128]{1,0:T(8,128)(2,1)}, bf16[256,128]{1,0:T(8,128)(2,1)}) custom-call(bf16[64,4096]{1,0:T(8,128)(2,1)S(1)} %get-tuple-element.22.refs_0_, bf16[256,128]{1,0:T(8,128)(2,1)S(1)} %get-tuple-element.23.refs_1_, bf16[256,128]{1,0:T(8,128)(2,1)S(1)} %get-tuple-element.24.refs_2_), custom_call_target="tpu_custom_call" | custom-call | tf_op jit(solution)/shard_map/hand_over/pallas_call | solution.py:774

commit v6 on v5

--- a/solution.py
+++ b/solution.py
@@ -17,9 +17,8 @@
 FAR_FIRST = (2, 1, 3, 0)
 RELAYED = (0, 1)
 GROUP = 4
-SCORES_AT_ONCE = 4
-GRADS_AT_ONCE = 2
-SLOTS = 26
+AT_ONCE = 4
+SLOTS = 24
 ROWS = 512
 SCALE = 1.0 / math.sqrt(D)
 LOG2E = math.log2(math.e)
@@ -382,6 +381,12 @@
     def fold(e):
         return jnp.sum(e.reshape(-1, 8, ROWS), axis=0)
 
+    def in_turns(turn, first, number):
+        whole = number // AT_ONCE
+        lax.fori_loop(0, whole, functools.partial(turn, first, AT_ONCE), 0)
+        done = whole * AT_ONCE
+        lax.fori_loop(0, (number - done + 1) // 2, functools.partial(turn, first + done, 2), 0)
+
     def one_half(half, carry):
         def pick(even, odd):
             return jnp.where(half == 0, even, odd)
@@ -441,9 +446,9 @@
             cut = jnp.where((query_at >= n0) & (starts[q] < n0), -NEG, 0.0)
             cuts[lines_of(q), :] = jnp.broadcast_to(top + cut, (8, ROWS))
 
-        def scores_turn(n, c):
-            for u in range(SCORES_AT_ONCE):
-                slot = 2 + n * SCORES_AT_ONCE + u
+        def scores_turn(first, width, n, c):
+            for u in range(width):
+                slot = first + n * width + u
                 q, g = item(slot)
                 blocks, real = blocks_of(q, g)
                 scores = lax.dot_general(gathered(0, blocks), qr[rows_of(half * 2 + q), :], NT,
@@ -458,7 +463,7 @@
                 inv[lines_of(q), :] += sums
             return c
 
-        lax.fori_loop(0, (items + SCORES_AT_ONCE - 1) // SCORES_AT_ONCE, scores_turn, 0)
+        in_turns(scores_turn, 2, items)
         totals = [jnp.sum(inv[q * 8:(q + 1) * 8, :], axis=0, keepdims=True) for q in range(2)]
         safe = jnp.max(jnp.maximum(totals[0], totals[1])) < 1e30
         for q in range(2):
@@ -493,10 +498,10 @@
             lax.fori_loop(0, items + 2, settle, 0)
             inv[...] = jnp.ones_like(inv)
 
-        def grads_turn(n, c):
+        def grads_turn(first, width, n, c):
             work = []
-            for u in range(GRADS_AT_ONCE):
-                slot = n * GRADS_AT_ONCE + u
+            for u in range(width):
+                slot = first + n * width + u
                 q, g = item(slot)
                 blocks, _ = blocks_of(q, g)
                 do_rows = dor[rows_of(half * 2 + q), :]
@@ -522,7 +527,7 @@
                     acc[1, rows, :] += dv[i * BLOCK:(i + 1) * BLOCK, :]
             return c
 
-        lax.fori_loop(0, (items + 2 + GRADS_AT_ONCE - 1) // GRADS_AT_ONCE, grads_turn, 0)
+        in_turns(grads_turn, 0, items + 2)
         return carry
 
     lax.fori_loop(0, 2, one_half, 0)
@@ -732,7 +737,7 @@
             pltpu.VMEM((4 * D, ROWS), F32),
             pltpu.SMEM((256,), jnp.int32), pltpu.SMEM((64,), jnp.int32), DMA,
         ],
-        compiler_params=pltpu.CompilerParams(vmem_limit_bytes=38 * MIB),
+        compiler_params=pltpu.CompilerParams(vmem_limit_bytes=42 * MIB),
         name="grads",
     )(parents, seg, q, do, dg, kv)
 

time: 70.8 us -> 71.7 us (1.013)
  the two profiles are of different devices: /device:TPU:10 before, /device:TPU:37 now
where the time goes in v6:
time: 71.7 us; the launch traced here: 70.4 us
  Pallas kernels  69.7 us (97%)
    pallas_call x1, Pallas kernels, home(): pl.pallas_call(home_kernel, out_shape=(pltpu.VMEM((64, 4096), BF16), pltp...  35.1 us
    pallas_call x1, Pallas kernels, spread(): pl.pallas_call(spread_kernel, out_shape=(pltpu.VMEM((COLUMN, ROWS), BF16)...  25.5 us
    pallas_call x1, Pallas kernels, grads(): pl.pallas_call(grad_kernel, out_shape=(pltpu.VMEM((2, NEAR, SECTION, D),...  8.37 us

profile of v6, /device:TPU:37, one launch (start us, length us, event | category | flops | bytes accessed | tf_op | source)
XLA Modules:
  0.0 70.4 jit_solution(2126947743544431400)
XLA Ops:
  0.6 25.5 %spread.1 = (bf16[512,512]{1,0:T(8,128)(2,1)S(1)}, bf16[512,512]{1,0:T(8,128)(2,1)S(1)}, f32[8,8,128]{2,1,0:T(8,128)S(1)}, bf16[2,8192,128]{2,1,0:T(8,128)(2,1)S...) custom-call(bf16[64,4096]{1,0:T(8,128)(2,1)} %q_ref.1, bf16[64,4096]{1,0:T(8,128)(2,1)} %do_ref.1, bf16[64,4096]{1,0:T(8,128)(2,1)} %o_ref.1, ...), custom_call_target="tpu_custom_call" | custom-call | tf_op jit(solution)/shard_map/spread/pallas_call | solution.py:704
  26.1 8.4 %grads.1 = (bf16[2,3,2048,128]{3,2,1,0:T(8,128)(2,1)S(1)}, bf16[512,512]{1,0:T(8,128)(2,1)S(1)}) custom-call(s32[64]{0:T(128)S(1)} %get-tuple-element.14.parents_near, s32[64,128]{1,0:T(8,128)S(1)} %get-tuple-element.15.seg_ref, bf16[512,512]{1,0:T(8,128)(2,1)S(1)} %get-tuple-element.16.q_all, bf16[512,512]{1,0:T(8,128)(2,1)S(1)} %get-tuple-element.17.do_all, ...), custom_call_target="tpu_custom_call" | custom-call | tf_op jit(solution)/shard_map/grads/pallas_call | solution.py:724
  34.5 35.1 %home.1 = (bf16[64,4096]{1,0:T(8,128)(2,1)S(1)}, bf16[256,128]{1,0:T(8,128)(2,1)S(1)}, bf16[256,128]{1,0:T(8,128)(2,1)S(1)}) custom-call(bf16[2,3,2048,128]{3,2,1,0:T(8,128)(2,1)S(1)} %get-tuple-element.20.dkv_ref, bf16[512,512]{1,0:T(8,128)(2,1)S(1)} %get-tuple-element.21.dq_ref), custom_call_target="tpu_custom_call" | custom-call | tf_op jit(solution)/shard_map/home/pallas_call | solution.py:746
  69.5 0.9 %hand_over.1 = (bf16[64,4096]{1,0:T(8,128)(2,1)}, bf16[256,128]{1,0:T(8,128)(2,1)}, bf16[256,128]{1,0:T(8,128)(2,1)}) custom-call(bf16[64,4096]{1,0:T(8,128)(2,1)S(1)} %get-tuple-element.22.refs_0_, bf16[256,128]{1,0:T(8,128)(2,1)S(1)} %get-tuple-element.23.refs_1_, bf16[256,128]{1,0:T(8,128)(2,1)S(1)} %get-tuple-element.24.refs_2_), custom_call_target="tpu_custom_call" | custom-call | tf_op jit(solution)/shard_map/hand_over/pallas_call | solution.py:779
